TPU v7x, 32 devices: a whole 2x2x4 slice. The times are simulated.
32 devices in a mesh: replica: 8 (over z, y), fsdp: 4 (over x, core).
Axes of the slice: x: 2, y: 2, z: 4, core: 2. Of those that a mesh axis runs over, the one named last changes fastest.
Arguments:
- activations: bfloat16 [8, 512, 8192], P('replica', 'fsdp'), may hold values from -6 to 6
- grad_out: bfloat16 [8, 512, 1024], P('replica', 'fsdp'), may hold values from -6 to 6
- local_weight: bfloat16 [8, 8192, 1024], P('replica', 'fsdp'), may hold values from -6 to 6
- anchor: float32 [8192, 1024], P('fsdp'), may hold values from -6 to 6
- momentum: float32 [8192, 256], P('fsdp'), may hold values from -6 to 6
- projection_key: int32 [2], replicated, may hold values from 0 to 1073741823
Outputs:
- new_anchor: float32 [8192, 1024], P('fsdp')
- new_momentum: float32 [8192, 256], P('fsdp')
All inputs are finite; a program needn't handle non-finite values.
Results may differ from a plain program's by a relative error of at most 0.0017.
Values may be sent and summed in bfloat16 or wider, within the bound.
A program may use at most 64 MiB of HBM per device.

v0:
```python
import jax
import jax.numpy as jnp
from jax import lax
from jax.sharding import PartitionSpec as P

HIGH = lax.Precision.HIGHEST


def projection(words, rows, cols):
    k_index = lax.broadcasted_iota(jnp.int32, (rows, cols), 0)
    r_index = lax.broadcasted_iota(jnp.int32, (rows, cols), 1)
    hashed = words[0] + k_index * 668265261 + r_index * 374761393 + words[1] * 1103515245
    hashed = jnp.bitwise_xor(hashed, lax.shift_right_logical(hashed, jnp.int32(15)))
    hashed = hashed * 739982445
    hashed = jnp.bitwise_xor(hashed, lax.shift_right_logical(hashed, jnp.int32(12)))
    hashed = hashed * 695938361
    hashed = jnp.bitwise_xor(hashed, lax.shift_right_logical(hashed, jnp.int32(15)))
    level = jnp.bitwise_and(lax.shift_right_logical(hashed, jnp.int32(8)), 65535).astype(
        jnp.float32
    )
    return ((level + 0.5) / 65536.0 - 0.5) * (12.0 / float(cols)) ** 0.5


def on_device(activations, grad_out, local_weight, anchor, momentum, projection_key):
    inputs = activations[0]
    grads = grad_out[0]
    local = local_weight[0]
    width_k = grads.shape[1]
    rank_cols = momentum.shape[1]
    proj = projection(projection_key, width_k, rank_cols)
    replicas = lax.axis_size("replica")
    scale = float(inputs.shape[0] * lax.axis_size("fsdp")) ** (-0.5)
    drift = anchor - local.astype(jnp.float32)
    columns = lax.all_to_all(inputs, "fsdp", split_axis=1, concat_axis=0, tiled=True)
    projected = jnp.dot(grads.astype(jnp.float32), proj, precision=HIGH)
    rows = columns.astype(jnp.float32)
    grad_part = lax.dot_general(
        rows,
        lax.all_gather(projected.astype(jnp.bfloat16), "fsdp", axis=0, tiled=True).astype(
            jnp.float32
        ),
        (((0,), (0,)), ((), ())),
        precision=HIGH,
        preferred_element_type=jnp.float32,
    )
    local_term = jnp.dot(drift, proj, precision=HIGH) + scale * grad_part
    summed = lax.psum(local_term, "replica")
    compressed_mean = summed / replicas
    new_momentum = 0.9 * momentum + compressed_mean
    update = compressed_mean + 0.9 * new_momentum
    new_anchor = anchor - 0.7 * jnp.dot(update, proj.T, precision=HIGH)
    return (new_anchor, new_momentum)


def solution(mesh):
    placed = (
        P("replica", "fsdp", None),
        P("replica", "fsdp", None),
        P("replica", "fsdp", None),
        P("fsdp", None),
        P("fsdp", None),
        P(),
    )
    return jax.shard_map(
        on_device,
        mesh=mesh,
        in_specs=placed,
        out_specs=(P("fsdp", None), P("fsdp", None)),
        check_vma=False,
    )
```

profile of v0, /device:TPU:0, one launch (start us, length us, event | category | flops | bytes accessed | tf_op | source)
XLA Modules:
  0.0 188.5 jit_solution(9265911358397058120)
XLA Ops:
  7.2 0.0 copy-start
  7.2 4.1 %copy.10 = bf16[1,128,8192]{1,2,0:T(8,128)(2,1)} copy(bf16[1,128,8192]{2,1,0:T(8,128)(2,1)} %param.6) | data formatting | bytes 4194304 | tf_op args[0]
  11.3 0.0 copy-start.5
  11.3 4.6 %all-to-all-start = ((bf16[128,4,2048]{0,2,1:T(8,128)(2,1)}), bf16[128,4,2048]{0,2,1:T(8,128)(2,1)}, u32[]{:S(2)}, u32[]{:S(2)}) async-start(bf16[128,4,2048]{0,2,1:T(8,128)(2,1)} %bitcast.5), calls=%async_computation | async-start | bytes 4194304 | tf_op jit(solution)/shard_map/all_to_all | solution.py:34
  15.9 0.0 all-reduce.2.cloned.1.call-start
  15.9 0.0 copy-done.5
  15.9 0.6 fusion.55
  17.3 0.7 multiply_add_fusion.1
  17.9 0.0 copy-done
  17.9 0.0 copy-start.3
  18.0 1.5 fusion.7
  19.5 24.9 %all_gather.3 = bf16[512,256]{0,1:T(8,128)(2,1)S(1)} all-gather(bf16[128,256]{0,1:T(8,128)(2,1)S(1)} %fusion.7), channel_id=1, replica_groups=mesh['replica'=8,'fsdp'=4] {'fsdp'}, dimensions={0}, use_global_device_ids=true | all-gather | bytes 327680 | tf_op jit(solution)/shard_map/all_gather | solution.py:39
  44.4 0.0 copy-done.3
  44.4 10.5 %fusion = f32[2048,256]{1,0:T(8,128)S(1)} fusion(f32[2048,1024]{1,0:T(8,128)} %param.9, bf16[1,2048,1024]{2,1,0:T(8,128)(2,1)S(1)} %copy-done.3, s32[]{:T(128)} %bitcast.2, s32[256]{0:T(256)S(1)} %iota_multiply_fusion, s32[1024]{0:T(1024)S(1)} %multiply_add_fusion.1), kind=kOutput, calls=%fused_computation.1 | convolution fusion | flops 6451101696 | bytes 14685188 | tf_op jit(solution)/shard_map/dot_general | solution.py:46
  54.9 0.0 all-to-all-done
  54.9 4.0 %copy.11 = bf16[4,128,2048]{2,1,0:T(8,128)(2,1)} copy(bf16[4,128,2048]{1,2,0:T(8,128)(2,1)} %bitcast.6) | data formatting | bytes 4194304 | tf_op jit(solution)/shard_map/all_to_all | solution.py:34
  58.8 3.8 %fusion.3 = f32[2048,256]{1,0:T(8,128)} fusion(f32[2048,256]{1,0:T(8,128)S(1)} %fusion, bf16[512,256]{0,1:T(8,128)(2,1)S(1)} %all_gather.3, bf16[512,2048]{1,0:T(8,128)(2,1)} %bitcast.22), kind=kOutput, calls=%fused_computation.6 | convolution fusion | flops 537919488 | bytes 6553600 | tf_op jit(solution)/shard_map/dot_general | solution.py:37
  62.7 0.0 copy-start.4
  62.7 0.0 all-reduce.2.cloned.1.call-update
  62.7 103.1 %all-reduce.2.cloned.1.call-done = f32[2048,256]{1,0:T(8,128)} async-done(((f32[2048,256]{1,0:T(8,128)}), f32[2048,256]{1,0:T(8,128)}) %all-reduce.2.cloned.1.call-update) | async-done | bytes 2097168 | tf_op jit(solution)/shard_map/psum | solution.py:47
  165.8 0.0 copy-done.4
  165.8 0.0 copy-start.1
  165.8 2.0 %multiply_add_fusion = f32[2048,256]{1,0:T(8,128)S(1)} fusion(f32[2048,256]{1,0:T(8,128)S(1)} %copy-done.4, f32[2048,256]{1,0:T(8,128)} %all-reduce.2.cloned.1.call-done), kind=kLoop, calls=%fused_computation.9 | loop fusion | flops 1572864 | bytes 6291456 | tf_op jit(solution)/shard_map/add | solution.py:49
  167.8 0.2 copy-done.1
  168.0 0.0 copy-start.2
  168.0 13.6 %multiply_subtract_fusion = f32[2048,1024]{1,0:T(8,128)} fusion(f32[2048,1024]{1,0:T(8,128)} %param.9, f32[2048,256]{1,0:T(8,128)S(1)} %multiply_add_fusion, f32[2048,256]{1,0:T(8,128)S(1)} %copy-done.1, s32[]{:T(128)} %bitcast.2, s32[256]{0:T(256)S(1)} %iota_multiply_fusion, s32[1024]{0:T(1024)S(1)} %multiply_add_fusion.1), kind=kOutput, calls=%fused_computation.2 | convolution fusion | flops 6452674560 | bytes 20976644 | tf_op jit(solution)/shard_map/dot_general | solution.py:51
  181.6 0.0 copy-done.2
  (1 shorter events, 0.0 us)
Async XLA Ops:
  7.2 10.8 %copy-start = (bf16[1,128,1024]{2,1,0:T(8,128)(2,1)S(1)}, bf16[1,128,1024]{2,1,0:T(8,128)(2,1)}, u32[]{:S(2)}) copy-start(bf16[1,128,1024]{2,1,0:T(8,128)(2,1)} %param.7) | copy-start | bytes 786436
  11.3 4.6 %copy-start.5 = (s32[2]{0:T(128)S(1)}, s32[2]{0:T(128)}, u32[]{:S(2)}) copy-start(s32[2]{0:T(128)} %param.11) | copy-start | bytes 28
  11.3 43.6 %all-to-all-start = ((bf16[128,4,2048]{0,2,1:T(8,128)(2,1)}), bf16[128,4,2048]{0,2,1:T(8,128)(2,1)}, u32[]{:S(2)}, u32[]{:S(2)}) async-start(bf16[128,4,2048]{0,2,1:T(8,128)(2,1)} %bitcast.5), calls=%async_computation | async-start | bytes 4194304 | tf_op jit(solution)/shard_map/all_to_all | solution.py:34
  15.9 149.9 %all-reduce.2.cloned.1.call-start = ((), (), s32[]{:S(2)}) async-start(), calls=%async_computation.1 | async-start | bytes 4194304 | tf_op jit(solution)/shard_map/psum | solution.py:47
  17.9 26.5 %copy-start.3 = (bf16[1,2048,1024]{2,1,0:T(8,128)(2,1)S(1)}, bf16[1,2048,1024]{2,1,0:T(8,128)(2,1)}, u32[]{:S(2)}) copy-start(bf16[1,2048,1024]{2,1,0:T(8,128)(2,1)} %param.8) | copy-start | bytes 12582916
  62.7 103.1 %copy-start.4 = (f32[2048,256]{1,0:T(8,128)S(1)}, f32[2048,256]{1,0:T(8,128)}, u32[]{:S(2)}) copy-start(f32[2048,256]{1,0:T(8,128)} %param.10) | copy-start | bytes 6291460
  165.8 2.2 %copy-start.1 = (f32[2048,256]{1,0:T(8,128)S(1)}, f32[2048,256]{1,0:T(8,128)}, u32[]{:S(2)}) copy-start(f32[2048,256]{1,0:T(8,128)} %all-reduce.2.cloned.1.call-done) | copy-start | bytes 6291460
  168.0 13.6 %copy-start.2 = (f32[2048,256]{1,0:T(8,128)}, f32[2048,256]{1,0:T(8,128)S(1)}, u32[]{:S(2)}) copy-start(f32[2048,256]{1,0:T(8,128)S(1)} %multiply_add_fusion) | copy-start | bytes 6291460
Sparse Core Ops, SparseCore 0:
  62.8 102.9 all-reduce.1
where the time goes:
time: 189 us; the launch traced here: 188 us
  waiting for transfers between devices  103 us (54%)
  matrix products  29.4 us (16%)
  blocking collectives  24.9 us (13%)
  between operations  14.8 us (8%)
  local copies, waits for them, and re-layouts  8.94 us (5%)
  starting transfers between devices  4.62 us (2%)
  other arithmetic  2.67 us (1%)
    psum x1, waiting for transfers between devices, on_device(): summed = lax.psum(local_term, 'replica')  103 us
    all_gather x1, blocking collectives, on_device(): lax.all_gather(projected.astype(jnp.bfloat16), 'fsdp', axis=0, tiled=True)  24.9 us
    dot_general x1, matrix products, on_device(): new_anchor = anchor - 0.7 * jnp.dot(update, proj.T, precision=HIGH)  13.6 us
    dot_general x1, matrix products, on_device(): local_term = jnp.dot(drift, proj, precision=HIGH) + scale * grad_part  10.5 us
    all_to_all x1, starting transfers between devices, on_device(): lax.all_to_all(inputs, 'fsdp', split_axis=1, concat_axis=0, tiled=True)  4.58 us
    unnamed x13, local copies, waits for them, and re-layouts  4.35 us
    all_to_all x1, local copies, waits for them, and re-layouts, on_device(): lax.all_to_all(inputs, 'fsdp', split_axis=1, concat_axis=0, tiled=True)  3.95 us
    dot_general x1, matrix products, on_device(): lax.dot_general(rows, lax.all_gather(projected.astype(jnp.bfloat16), 'fsd...  3.85 us
  transfers between devices with their start and end apart: 2, of which 1 were waited for; matrix products, arithmetic and copies ran while one was open for 7% of the time, Pallas kernels for 0%

commit v1 on v0

v1 whole, which is shorter than its diff:
```python
import functools

import jax
import jax.numpy as jnp
from jax import lax
from jax.experimental import pallas as pl
from jax.experimental.pallas import tpu as pltpu
from jax.sharding import PartitionSpec as P

HIGH = lax.Precision.HIGHEST
MESH = pl.DeviceIdType.MESH
CHUNKS = 4
PAD = 16
LEVELS = 32500.0
STEPS = 256.0
NT = (((1,), (1,)), ((), ()))
TN = (((0,), (0,)), ((), ()))


def projection(word0, word1, rows, cols, first=0):
    k_index = lax.broadcasted_iota(jnp.int32, (rows, cols), 0) + first
    r_index = lax.broadcasted_iota(jnp.int32, (rows, cols), 1)
    hashed = word0 + k_index * 668265261 + r_index * 374761393 + word1 * 1103515245
    hashed = jnp.bitwise_xor(hashed, lax.shift_right_logical(hashed, jnp.int32(15)))
    hashed = hashed * 739982445
    hashed = jnp.bitwise_xor(hashed, lax.shift_right_logical(hashed, jnp.int32(12)))
    hashed = hashed * 695938361
    hashed = jnp.bitwise_xor(hashed, lax.shift_right_logical(hashed, jnp.int32(15)))
    level = jnp.bitwise_and(lax.shift_right_logical(hashed, jnp.int32(8)), 65535).astype(
        jnp.float32
    )
    return ((level + 0.5) / 65536.0 - 0.5) * (12.0 / float(cols)) ** 0.5


def split(value):
    high = value.astype(jnp.bfloat16)
    return high, (value - high.astype(jnp.float32)).astype(jnp.bfloat16)


def dot(a, b, dims=(((1,), (0,)), ((), ()))):
    return lax.dot_general(a, b, dims, preferred_element_type=jnp.float32)


def encode(value, ref):
    rows = value.shape[0]
    top = jnp.max(jnp.abs(value), axis=0, keepdims=True)
    power = jnp.ceil(jnp.log(jnp.maximum(top, 1e-30)) * (STEPS * 1.4426950408889634))
    factor = jnp.exp2(power * (-1.0 / STEPS)) * LEVELS
    ref[:rows, :] = jnp.round(value * factor).astype(jnp.int32).astype(jnp.int16)
    ref[rows:, :] = jnp.broadcast_to(
        power.astype(jnp.int32), (PAD, value.shape[1])
    ).astype(jnp.int16)


def decode(ref):
    rows = ref.shape[0] - PAD
    power = ref[rows:, :].astype(jnp.int32).astype(jnp.float32)[:1]
    scale = jnp.exp2(power * (1.0 / STEPS)) * (1.0 / LEVELS)
    return ref[:rows, :].astype(jnp.int32).astype(jnp.float32) * scale


def mean_kernel(
    n_rep, n_y, n_f, key, act, grads, local, anchor, gathered, proj,
    columns, weights, own_anchor, total, pg, grads_in, y_out, y_in, z_out, z_in,
    act_s, act_r, pg_s, pg_r, y1_s, y1_r, z1_s, z1_r, z2_s, z2_r, y2_s, y2_r, here,
):
    n_z = n_rep // n_y
    chunks, tokens_all, width = columns.shape
    tokens = tokens_all // n_f
    half = width // n_y
    block = half // n_z
    depth = weights.shape[2]
    rank = pg.shape[1]
    rep = lax.axis_index("replica")
    f = lax.axis_index("fsdp")
    z, y = rep // n_y, rep % n_y
    other = n_y - 1 - y
    y_peer = {"replica": z * n_y + other}

    def z_peer(d):
        return {"replica": ((z + d) % n_z) * n_y + y}

    barrier = pltpu.get_barrier_semaphore()
    for d in range(1, n_f):
        pl.semaphore_signal(barrier, inc=1, device_id={"fsdp": (f + d) % n_f}, device_id_type=MESH)
    for d in range(1, n_z):
        pl.semaphore_signal(barrier, inc=1, device_id=z_peer(d), device_id_type=MESH)
    pl.semaphore_signal(barrier, inc=1, device_id=y_peer, device_id_type=MESH)

    def remote(src, dst, send, recv, device):
        return pltpu.make_async_remote_copy(
            src_ref=src, dst_ref=dst, send_sem=send, recv_sem=recv,
            device_id=device, device_id_type=MESH,
        )

    mine = pl.ds(pl.multiple_of(f * tokens, tokens), tokens)

    def act_copy(c, d):
        g = (f + d) % n_f
        at = pl.ds(pl.multiple_of((g * chunks + c) * width, width), width)
        return remote(
            act.at[0, :, at], columns.at[c, mine, :], act_s.at[c, d - 1], act_r.at[c, d - 1],
            {"fsdp": g},
        )

    def act_own(c):
        at = pl.ds(pl.multiple_of((f * chunks + c) * width, width), width)
        return pltpu.make_async_copy(act.at[0, :, at], columns.at[c, mine, :], here.at[0, c])

    def weight_copy(c):
        at = pl.ds(pl.multiple_of(c * width, width), width)
        return pltpu.make_async_copy(local.at[0, at, :], weights.at[c], here.at[1, c])

    def anchor_copy(c):
        at = pl.ds(pl.multiple_of(c * width + y * half + z * block, block), block)
        return pltpu.make_async_copy(anchor.at[at, :], own_anchor.at[c], here.at[2, c])

    def pg_copy(d):
        return remote(
            pg.at[mine, :], pg.at[mine, :], pg_s.at[d - 1], pg_r.at[d - 1], {"fsdp": (f + d) % n_f}
        )

    def y1_copy(c):
        return remote(y_out.at[c], y_in.at[c], y1_s.at[c], y1_r.at[c], y_peer)

    def z1_copy(c, d):
        return remote(
            z_out.at[c, d - 1], z_in.at[c, d - 1], z1_s.at[c, d - 1], z1_r.at[c, d - 1], z_peer(d)
        )

    def z2_copy(c, d):
        return remote(
            gathered.at[c, y, z], gathered.at[c, y, z], z2_s.at[c, d - 1], z2_r.at[c, d - 1],
            z_peer(d),
        )

    def y2_copy(c):
        return remote(gathered.at[c, y], gathered.at[c, y], y2_s.at[c], y2_r.at[c], y_peer)

    fetch = pltpu.make_async_copy(grads.at[0], grads_in, here.at[3, 0])
    fetch.start()
    for c in range(chunks):
        weight_copy(c).start()
        act_own(c).start()
        anchor_copy(c).start()
    pl.semaphore_wait(barrier, n_f + n_z - 1)
    order = sorted(range(1, n_f), key=lambda d: abs(d - n_f // 2))
    for d in order:
        act_copy(0, d).start()

    @pl.loop(0, depth, step=rank)
    def _(k):
        at = pl.ds(pl.multiple_of(k, rank), rank)
        high, low = split(projection(key[0], key[1], rank, rank, k))
        proj[at, :rank] = high
        proj[at, rank:] = low

    fetch.wait()
    both = dot(grads_in[...], proj[...])
    pg[mine, :] = (both[:, :rank] + both[:, rank:]).astype(jnp.bfloat16)
    for d in order:
        pg_copy(d).start()
    for c in range(1, chunks):
        for d in order:
            act_copy(c, d).start()

    @pl.loop(0, chunks)
    def _(c):
        weight_copy(c).wait()
        for h in range(n_y):
            at = pl.ds(h * half, half)
            both = dot(weights[c, at, :], proj[...])
            total[c, at, :] = (both[:, :rank] + both[:, rank:]) * (-1.0 / n_rep)

    for d in range(1, n_f):
        pg_copy(d).wait_recv()
    scale = float(tokens_all) ** (-0.5) / n_rep

    @pl.loop(0, chunks + 3)
    def _(t):
        @pl.when(t < chunks)
        def _():
            c = t
            act_own(c).wait()
            for d in range(1, n_f):
                act_copy(c, d).wait_recv()
            total[c] += dot(columns[c], pg[...], TN) * scale
            far = pl.ds(pl.multiple_of(other * half, half), half)
            encode(total[c, far, :], y_out.at[c])
            y1_copy(c).start()

        @pl.when(jnp.logical_and(t >= 1, t < chunks + 1))
        def _():
            c = t - 1
            y1_copy(c).wait_recv()
            near = pl.ds(pl.multiple_of(y * half, half), half)
            total[c, near, :] += decode(y_in.at[c])
            for d in range(1, n_z):
                q = (z + d) % n_z
                at = pl.ds(pl.multiple_of(y * half + q * block, block), block)
                encode(total[c, at, :], z_out.at[c, d - 1])
                z1_copy(c, d).start()

        @pl.when(jnp.logical_and(t >= 2, t < chunks + 2))
        def _():
            c = t - 2
            at = pl.ds(pl.multiple_of(y * half + z * block, block), block)
            anchor_copy(c).wait()
            high, low = split(own_anchor[c])
            both = dot(high, proj[...])
            value = total[c, at, :] + both[:, :rank] + both[:, rank:] + dot(low, proj[:, :rank])
            for d in range(1, n_z):
                z1_copy(c, d).wait_recv()
                value += decode(z_in.at[c, d - 1])
            encode(value, gathered.at[c, y, z])
            for d in range(1, n_z):
                z2_copy(c, d).start()

        @pl.when(t >= 3)
        def _():
            c = t - 3
            for d in range(1, n_z):
                z2_copy(c, d).wait_recv()
            y2_copy(c).start()

    for d in range(1, n_f):
        pg_copy(d).wait_send()

    @pl.loop(0, chunks)
    def _(c):
        for d in range(1, n_f):
            act_copy(c, d).wait_send()
        y1_copy(c).wait_send()
        for d in range(1, n_z):
            z1_copy(c, d).wait_send()
            z2_copy(c, d).wait_send()
        y2_copy(c).wait_send()
        y2_copy(c).wait_recv()


def update_kernel(gathered, proj, anchor, momentum, new_anchor, new_momentum):
    n_z, block = gathered.shape[2], gathered.shape[3] - PAD
    rank = momentum.shape[1]
    for q in range(n_z):
        at = pl.ds(q * block, block)
        mean = decode(gathered.at[0, 0, q])
        moved = 0.9 * momentum[at, :] + mean
        new_momentum[at, :] = moved
    mean = new_momentum[...] - 0.9 * momentum[...]
    high, low = split(mean + 0.9 * new_momentum[...])
    step = dot(high, proj[:, :rank], NT) + dot(high, proj[:, rank:], NT)
    step += dot(low, proj[:, :rank], NT)
    new_anchor[...] = anchor[...] - 0.7 * step


def in_kernels(n_rep, n_y, n_f, act, grads, local, anchor, momentum, key):
    n_z = n_rep // n_y
    rows, depth = anchor.shape
    rank = momentum.shape[1]
    tokens = act.shape[1]
    width = rows // CHUNKS
    half = width // n_y
    block = half // n_z
    dma = pltpu.SemaphoreType.DMA
    any_space = pl.BlockSpec(memory_space=pl.ANY)
    vmem = pl.BlockSpec(memory_space=pltpu.VMEM)
    gathered, proj = pl.pallas_call(
        functools.partial(mean_kernel, n_rep, n_y, n_f),
        out_shape=(
            jax.ShapeDtypeStruct((CHUNKS, n_y, n_z, block + PAD, rank), jnp.int16),
            jax.ShapeDtypeStruct((depth, 2 * rank), jnp.bfloat16),
        ),
        in_specs=[pl.BlockSpec(memory_space=pltpu.SMEM)] + [any_space] * 4,
        out_specs=(vmem, vmem),
        scratch_shapes=[
            pltpu.VMEM((CHUNKS, tokens * n_f, width), jnp.bfloat16),
            pltpu.VMEM((CHUNKS, width, depth), jnp.bfloat16),
            pltpu.VMEM((CHUNKS, block, depth), jnp.float32),
            pltpu.VMEM((CHUNKS, width, rank), jnp.float32),
            pltpu.VMEM((tokens * n_f, rank), jnp.bfloat16),
            pltpu.VMEM((tokens, depth), jnp.bfloat16),
            pltpu.VMEM((CHUNKS, half + PAD, rank), jnp.int16),
            pltpu.VMEM((CHUNKS, half + PAD, rank), jnp.int16),
            pltpu.VMEM((CHUNKS, n_z - 1, block + PAD, rank), jnp.int16),
            pltpu.VMEM((CHUNKS, n_z - 1, block + PAD, rank), jnp.int16),
            dma((CHUNKS, n_f - 1)),
            dma((CHUNKS, n_f - 1)),
            dma((n_f - 1,)),
            dma((n_f - 1,)),
            dma((CHUNKS,)),
            dma((CHUNKS,)),
            dma((CHUNKS, n_z - 1)),
            dma((CHUNKS, n_z - 1)),
            dma((CHUNKS, n_z - 1)),
            dma((CHUNKS, n_z - 1)),
            dma((CHUNKS,)),
            dma((CHUNKS,)),
            dma((4, CHUNKS)),
        ],
        compiler_params=pltpu.CompilerParams(
            collective_id=0, has_side_effects=True, vmem_limit_bytes=40 * 1024 * 1024
        ),
        name="mean",
    )(key, act, grads, local, anchor)

    def tile(i):
        return (i, 0)

    return pl.pallas_call(
        update_kernel,
        grid=(CHUNKS * n_y,),
        out_shape=(
            jax.ShapeDtypeStruct(anchor.shape, anchor.dtype),
            jax.ShapeDtypeStruct(momentum.shape, momentum.dtype),
        ),
        in_specs=[
            pl.BlockSpec((1, 1, n_z, block + PAD, rank), lambda i: (i // n_y, i % n_y, 0, 0, 0)),
            pl.BlockSpec((depth, 2 * rank), lambda i: (0, 0)),
            pl.BlockSpec((half, depth), tile),
            pl.BlockSpec((half, rank), tile),
        ],
        out_specs=(pl.BlockSpec((half, depth), tile), pl.BlockSpec((half, rank), tile)),
        compiler_params=pltpu.CompilerParams(vmem_limit_bytes=32 * 1024 * 1024),
        name="update",
    )(gathered, proj, anchor, momentum)


def in_steps(activations, grad_out, local_weight, anchor, momentum, projection_key):
    inputs = activations[0]
    grads = grad_out[0]
    local = local_weight[0]
    proj = projection(projection_key[0], projection_key[1], grads.shape[1], momentum.shape[1])
    replicas = lax.axis_size("replica")
    scale = float(inputs.shape[0] * lax.axis_size("fsdp")) ** (-0.5)
    drift = anchor - local.astype(jnp.float32)
    columns = lax.all_to_all(inputs, "fsdp", split_axis=1, concat_axis=0, tiled=True)
    projected = jnp.dot(grads.astype(jnp.float32), proj, precision=HIGH)
    grad_part = lax.dot_general(
        columns.astype(jnp.float32),
        lax.all_gather(projected.astype(jnp.bfloat16), "fsdp", axis=0, tiled=True).astype(
            jnp.float32
        ),
        TN,
        precision=HIGH,
        preferred_element_type=jnp.float32,
    )
    local_term = jnp.dot(drift, proj, precision=HIGH) + scale * grad_part
    compressed_mean = lax.psum(local_term, "replica") / replicas
    new_momentum = 0.9 * momentum + compressed_mean
    update = compressed_mean + 0.9 * new_momentum
    new_anchor = anchor - 0.7 * jnp.dot(update, proj.T, precision=HIGH)
    return (new_anchor, new_momentum)


def solution(mesh):
    n_rep, n_f = mesh.shape["replica"], mesh.shape["fsdp"]
    n_y = 2

    def on_device(act, grads, local, anchor, momentum, key):
        rows, depth = anchor.shape
        rank = momentum.shape[1]
        fits = n_rep % n_y == 0 and n_rep > n_y and n_f > 1
        fits = fits and rows % (CHUNKS * n_rep * 16) == 0 and (rows // CHUNKS) % 128 == 0
        fits = fits and act.shape[1] % 16 == 0 and rank % 128 == 0 and depth % rank == 0
        if fits:
            return in_kernels(n_rep, n_y, n_f, act, grads, local, anchor, momentum, key)
        return in_steps(act, grads, local, anchor, momentum, key)

    placed = (
        P("replica", "fsdp", None),
        P("replica", "fsdp", None),
        P("replica", "fsdp", None),
        P("fsdp", None),
        P("fsdp", None),
        P(),
    )
    return jax.shard_map(
        on_device,
        mesh=mesh,
        in_specs=placed,
        out_specs=(P("fsdp", None), P("fsdp", None)),
        check_vma=False,
    )
```

time: 189 us -> 71.6 us (0.38)
  the two profiles are of different devices: /device:TPU:0 before, /device:TPU:11 now
where the time goes in v1:
time: 71.6 us; the launch traced here: 71.4 us
  Pallas kernels  65.3 us (91%)
  local copies, waits for them, and re-layouts  5.38 us (8%)
    pallas_call x1, Pallas kernels, in_kernels(): pl.pallas_call(functools.partial(mean_kernel, n_rep, n_y, n_f), out_shape...  58.3 us
    pallas_call x1, Pallas kernels, in_kernels(): pl.pallas_call(update_kernel, grid=(CHUNKS * n_y,), out_shape=(jax.ShapeD...  7.04 us
    unnamed x12, local copies, waits for them, and re-layouts  5.38 us

profile of v1, /device:TPU:11, one launch (start us, length us, event | category | flops | bytes accessed | tf_op | source)
XLA Modules:
  0.0 71.4 jit_solution(16865028972004266236)
XLA Ops:
  0.6 0.0 copy-start.1
  0.6 2.2 %copy-done.1 = bf16[1,2048,1024]{2,1,0:T(8,128)(2,1)S(1)} copy-done((bf16[1,2048,1024]{2,1,0:T(8,128)(2,1)S(1)}, bf16[1,2048,1024]{2,1,0:T(8,128)(2,1)}, u32[]{:S(2)}) %copy-start.1) | copy-done | bytes 4194328
  2.8 0.0 copy-start.3
  2.8 1.6 %copy-done.3 = bf16[1,128,8192]{2,1,0:T(8,128)(2,1)S(1)} copy-done((bf16[1,128,8192]{2,1,0:T(8,128)(2,1)S(1)}, bf16[1,128,8192]{2,1,0:T(8,128)(2,1)}, u32[]{:S(2)}) %copy-start.3) | copy-done | bytes 2097176
  4.4 0.0 copy-start.4
  4.4 0.9 %copy-done.4 = bf16[1,128,1024]{2,1,0:T(8,128)(2,1)S(1)} copy-done((bf16[1,128,1024]{2,1,0:T(8,128)(2,1)S(1)}, bf16[1,128,1024]{2,1,0:T(8,128)(2,1)}, u32[]{:S(2)}) %copy-start.4) | copy-done | bytes 262168
  5.4 0.0 copy-start.5
  5.4 0.7 copy-done.5
  6.0 0.0 copy-start
  6.0 0.0 copy-start.2
  6.0 58.3 %mean.1 = (s16[4,2,4,80,256]{4,3,2,1,0:T(8,128)(2,1)S(1)}, bf16[1024,512]{1,0:T(8,128)(2,1)S(1)}) custom-call(s32[2]{0:T(128)S(1)} %copy-done.5, bf16[1,128,8192]{2,1,0:T(8,128)(2,1)S(1)} %copy-done.3, bf16[1,128,1024]{2,1,0:T(8,128)(2,1)S(1)} %copy-done.4, bf16[1,2048,1024]{2,1,0:T(8,128)(2,1)S(1)} %copy-done.1, f32[2048,1024]{1,0:T(8,128)} %anchor.3), custom_call_target="tpu_custom_call" | custom-call | tf_op jit(solution)/shard_map/mean/pallas_call | solution.py:267
  64.3 0.0 copy-done
  64.3 0.0 copy-done.2
  64.3 7.0 %update.1 = (f32[2048,1024]{1,0:T(8,128)}, f32[2048,256]{1,0:T(8,128)}) custom-call(s16[4,2,4,80,256]{4,3,2,1,0:T(8,128)(2,1)S(1)} %get-tuple-element.4.gathered, bf16[1024,512]{1,0:T(8,128)(2,1)S(1)} %get-tuple-element.5.proj, f32[2048,1024]{1,0:T(8,128)S(1)} %copy-done, f32[2048,256]{1,0:T(8,128)S(1)} %copy-done.2), custom_call_target="tpu_custom_call" | custom-call | tf_op jit(solution)/shard_map/update/pallas_call | solution.py:309
Async XLA Ops:
  0.6 2.2 %copy-start.1 = (bf16[1,2048,1024]{2,1,0:T(8,128)(2,1)S(1)}, bf16[1,2048,1024]{2,1,0:T(8,128)(2,1)}, u32[]{:S(2)}) copy-start(bf16[1,2048,1024]{2,1,0:T(8,128)(2,1)} %local.1) | copy-start | bytes 12582916
  2.8 1.6 %copy-start.3 = (bf16[1,128,8192]{2,1,0:T(8,128)(2,1)S(1)}, bf16[1,128,8192]{2,1,0:T(8,128)(2,1)}, u32[]{:S(2)}) copy-start(bf16[1,128,8192]{2,1,0:T(8,128)(2,1)} %act.1) | copy-start | bytes 6291460
  4.4 0.9 %copy-start.4 = (bf16[1,128,1024]{2,1,0:T(8,128)(2,1)S(1)}, bf16[1,128,1024]{2,1,0:T(8,128)(2,1)}, u32[]{:S(2)}) copy-start(bf16[1,128,1024]{2,1,0:T(8,128)(2,1)} %grads.1) | copy-start | bytes 786436
  5.4 0.7 copy-start.5
  6.0 58.3 %copy-start = (f32[2048,1024]{1,0:T(8,128)S(1)}, f32[2048,1024]{1,0:T(8,128)}, u32[]{:S(2)}) copy-start(f32[2048,1024]{1,0:T(8,128)} %anchor.3) | copy-start | bytes 25165828
  6.0 58.3 %copy-start.2 = (f32[2048,256]{1,0:T(8,128)S(1)}, f32[2048,256]{1,0:T(8,128)}, u32[]{:S(2)}) copy-start(f32[2048,256]{1,0:T(8,128)} %momentum.1) | copy-start | bytes 6291460

commit v2 on v1

--- a/solution.py
+++ b/solution.py
@@ -11,6 +11,7 @@
 MESH = pl.DeviceIdType.MESH
 CHUNKS = 4
 PAD = 16
+LANES = 128
 LEVELS = 32500.0
 STEPS = 256.0
 NT = (((1,), (1,)), ((), ()))
@@ -42,26 +43,38 @@
 
 
 def encode(value, ref):
-    rows = value.shape[0]
+    rows, cols = value.shape
     top = jnp.max(jnp.abs(value), axis=0, keepdims=True)
     power = jnp.ceil(jnp.log(jnp.maximum(top, 1e-30)) * (STEPS * 1.4426950408889634))
     factor = jnp.exp2(power * (-1.0 / STEPS)) * LEVELS
-    ref[:rows, :] = jnp.round(value * factor).astype(jnp.int32).astype(jnp.int16)
-    ref[rows:, :] = jnp.broadcast_to(
-        power.astype(jnp.int32), (PAD, value.shape[1])
-    ).astype(jnp.int16)
-
-
-def decode(ref):
-    rows = ref.shape[0] - PAD
-    power = ref[rows:, :].astype(jnp.int32).astype(jnp.float32)[:1]
+    coded = jnp.round(value * factor).astype(jnp.int32).astype(jnp.int16)
+    line = lax.broadcasted_iota(jnp.int32, (PAD, LANES), 0)
+    scales = jnp.zeros((PAD, LANES), jnp.float32)
+    for part in range(cols // LANES):
+        at = slice(part * LANES, (part + 1) * LANES)
+        ref[part * rows : (part + 1) * rows, :] = coded[:, at]
+        scales = jnp.where(line == part, power[:, at], scales)
+    ref[cols // LANES * rows :, :] = scales.astype(jnp.int32).astype(jnp.int16)
+
+
+def decode(ref, cols):
+    parts = cols // LANES
+    rows = (ref.shape[0] - PAD) // parts
+    power = ref[parts * rows :, :].astype(jnp.int32).astype(jnp.float32)
     scale = jnp.exp2(power * (1.0 / STEPS)) * (1.0 / LEVELS)
-    return ref[:rows, :].astype(jnp.int32).astype(jnp.float32) * scale
+    return jnp.concatenate(
+        [
+            ref[part * rows : (part + 1) * rows, :].astype(jnp.int32).astype(jnp.float32)
+            * scale[part : part + 1]
+            for part in range(parts)
+        ],
+        axis=1,
+    )
 
 
 def mean_kernel(
-    n_rep, n_y, n_f, key, act, grads, local, anchor, gathered, proj,
-    columns, weights, own_anchor, total, pg, grads_in, y_out, y_in, z_out, z_in,
+    n_rep, n_y, n_f, key_hbm, act, grads, local, anchor, gathered, proj,
+    key, columns, weights, own_anchor, total, pg, grads_in, y_out, y_in, z_out, z_in,
     act_s, act_r, pg_s, pg_r, y1_s, y1_r, z1_s, z1_r, z2_s, z2_r, y2_s, y2_r, here,
 ):
     n_z = n_rep // n_y
@@ -139,6 +152,8 @@
 
     fetch = pltpu.make_async_copy(grads.at[0], grads_in, here.at[3, 0])
     fetch.start()
+    words = pltpu.make_async_copy(key_hbm, key, here.at[3, 1])
+    words.start()
     for c in range(chunks):
         weight_copy(c).start()
         act_own(c).start()
@@ -147,6 +162,7 @@
     order = sorted(range(1, n_f), key=lambda d: abs(d - n_f // 2))
     for d in order:
         act_copy(0, d).start()
+    words.wait()
 
     @pl.loop(0, depth, step=rank)
     def _(k):
@@ -160,9 +176,8 @@
     pg[mine, :] = (both[:, :rank] + both[:, rank:]).astype(jnp.bfloat16)
     for d in order:
         pg_copy(d).start()
-    for c in range(1, chunks):
-        for d in order:
-            act_copy(c, d).start()
+    for d in order:
+        act_copy(1, d).start()
 
     @pl.loop(0, chunks)
     def _(c):
@@ -176,52 +191,58 @@
         pg_copy(d).wait_recv()
     scale = float(tokens_all) ** (-0.5) / n_rep
 
-    @pl.loop(0, chunks + 3)
+    def partial_sum(c):
+        act_own(c).wait()
+        for d in range(1, n_f):
+            act_copy(c, d).wait_recv()
+
+        @pl.when(c + 2 < chunks)
+        def _():
+            for d in order:
+                act_copy(c + 2, d).start()
+
+        total[c] += dot(columns[c], pg[...], TN) * scale
+        far = pl.ds(pl.multiple_of(other * half, half), half)
+        encode(total[c, far, :], y_out.at[c])
+        y1_copy(c).start()
+
+    def sum_of_pair(c):
+        y1_copy(c).wait_recv()
+        near = pl.ds(pl.multiple_of(y * half, half), half)
+        total[c, near, :] += decode(y_in.at[c], rank)
+        for d in range(1, n_z):
+            q = (z + d) % n_z
+            at = pl.ds(pl.multiple_of(y * half + q * block, block), block)
+            encode(total[c, at, :], z_out.at[c, d - 1])
+            z1_copy(c, d).start()
+
+    def whole_mean(c):
+        at = pl.ds(pl.multiple_of(y * half + z * block, block), block)
+        anchor_copy(c).wait()
+        high, low = split(own_anchor[c])
+        both = dot(high, proj[...])
+        value = total[c, at, :] + both[:, :rank] + both[:, rank:] + dot(low, proj[:, :rank])
+        for d in range(1, n_z):
+            z1_copy(c, d).wait_recv()
+            value += decode(z_in.at[c, d - 1], rank)
+        encode(value, gathered.at[c, y, z])
+        for d in range(1, n_z):
+            z2_copy(c, d).start()
+
+    def hand_over(c):
+        for d in range(1, n_z):
+            z2_copy(c, d).wait_recv()
+        y2_copy(c).start()
+
+    stages = ((partial_sum, 0), (hand_over, 2), (whole_mean, 1), (sum_of_pair, 0))
+
+    @pl.loop(0, chunks + 2)
     def _(t):
-        @pl.when(t < chunks)
-        def _():
-            c = t
-            act_own(c).wait()
-            for d in range(1, n_f):
-                act_copy(c, d).wait_recv()
-            total[c] += dot(columns[c], pg[...], TN) * scale
-            far = pl.ds(pl.multiple_of(other * half, half), half)
-            encode(total[c, far, :], y_out.at[c])
-            y1_copy(c).start()
-
-        @pl.when(jnp.logical_and(t >= 1, t < chunks + 1))
-        def _():
-            c = t - 1
-            y1_copy(c).wait_recv()
-            near = pl.ds(pl.multiple_of(y * half, half), half)
-            total[c, near, :] += decode(y_in.at[c])
-            for d in range(1, n_z):
-                q = (z + d) % n_z
-                at = pl.ds(pl.multiple_of(y * half + q * block, block), block)
-                encode(total[c, at, :], z_out.at[c, d - 1])
-                z1_copy(c, d).start()
-
-        @pl.when(jnp.logical_and(t >= 2, t < chunks + 2))
-        def _():
-            c = t - 2
-            at = pl.ds(pl.multiple_of(y * half + z * block, block), block)
-            anchor_copy(c).wait()
-            high, low = split(own_anchor[c])
-            both = dot(high, proj[...])
-            value = total[c, at, :] + both[:, :rank] + both[:, rank:] + dot(low, proj[:, :rank])
-            for d in range(1, n_z):
-                z1_copy(c, d).wait_recv()
-                value += decode(z_in.at[c, d - 1])
-            encode(value, gathered.at[c, y, z])
-            for d in range(1, n_z):
-                z2_copy(c, d).start()
-
-        @pl.when(t >= 3)
-        def _():
-            c = t - 3
-            for d in range(1, n_z):
-                z2_copy(c, d).wait_recv()
-            y2_copy(c).start()
+        for stage, lag in stages:
+
+            @pl.when(jnp.logical_and(t >= lag, t < chunks + lag))
+            def _(stage=stage, lag=lag):
+                stage(t - lag)
 
     for d in range(1, n_f):
         pg_copy(d).wait_send()
@@ -238,19 +259,47 @@
         y2_copy(c).wait_recv()
 
 
-def update_kernel(gathered, proj, anchor, momentum, new_anchor, new_momentum):
-    n_z, block = gathered.shape[2], gathered.shape[3] - PAD
+def update_kernel(
+    gathered, proj, anchor, momentum, new_anchor, new_momentum, anchor_out, momentum_out, sems
+):
+    chunks, n_y, n_z = gathered.shape[:3]
     rank = momentum.shape[1]
-    for q in range(n_z):
-        at = pl.ds(q * block, block)
-        mean = decode(gathered.at[0, 0, q])
+    width = momentum.shape[0] // chunks
+    block = width // n_y // n_z
+
+    def stores(c):
+        at = pl.ds(pl.multiple_of(c * width, width), width)
+        slot = c % 2
+        return (
+            pltpu.make_async_copy(anchor_out.at[slot], new_anchor.at[at, :], sems.at[0, slot]),
+            pltpu.make_async_copy(momentum_out.at[slot], new_momentum.at[at, :], sems.at[1, slot]),
+        )
+
+    @pl.loop(0, chunks)
+    def _(c):
+        slot = c % 2
+
+        @pl.when(c >= 2)
+        def _():
+            for store in stores(c - 2):
+                store.wait()
+
+        mean = jnp.concatenate(
+            [decode(gathered.at[c, h, q], rank) for h in range(n_y) for q in range(n_z)], axis=0
+        )
+        at = pl.ds(pl.multiple_of(c * width, width), width)
         moved = 0.9 * momentum[at, :] + mean
-        new_momentum[at, :] = moved
-    mean = new_momentum[...] - 0.9 * momentum[...]
-    high, low = split(mean + 0.9 * new_momentum[...])
-    step = dot(high, proj[:, :rank], NT) + dot(high, proj[:, rank:], NT)
-    step += dot(low, proj[:, :rank], NT)
-    new_anchor[...] = anchor[...] - 0.7 * step
+        momentum_out[slot] = moved
+        high, low = split(mean + 0.9 * moved)
+        step = dot(jnp.concatenate([high, high], axis=1), proj[...], NT)
+        step += dot(low, proj[:, :rank], NT)
+        anchor_out[slot] = anchor[at, :] - 0.7 * step
+        for store in stores(c):
+            store.start()
+
+    for c in range(max(chunks - 2, 0), chunks):
+        for store in stores(c):
+            store.wait()
 
 
 def in_kernels(n_rep, n_y, n_f, act, grads, local, anchor, momentum, key):
@@ -262,27 +311,29 @@
     half = width // n_y
     block = half // n_z
     dma = pltpu.SemaphoreType.DMA
-    any_space = pl.BlockSpec(memory_space=pl.ANY)
+    hbm = pl.BlockSpec(memory_space=pltpu.HBM)
+    coded = rank // LANES
     vmem = pl.BlockSpec(memory_space=pltpu.VMEM)
     gathered, proj = pl.pallas_call(
         functools.partial(mean_kernel, n_rep, n_y, n_f),
         out_shape=(
-            jax.ShapeDtypeStruct((CHUNKS, n_y, n_z, block + PAD, rank), jnp.int16),
+            jax.ShapeDtypeStruct((CHUNKS, n_y, n_z, coded * block + PAD, LANES), jnp.int16),
             jax.ShapeDtypeStruct((depth, 2 * rank), jnp.bfloat16),
         ),
-        in_specs=[pl.BlockSpec(memory_space=pltpu.SMEM)] + [any_space] * 4,
+        in_specs=[hbm] * 5,
         out_specs=(vmem, vmem),
         scratch_shapes=[
+            pltpu.SMEM(key.shape, jnp.int32),
             pltpu.VMEM((CHUNKS, tokens * n_f, width), jnp.bfloat16),
             pltpu.VMEM((CHUNKS, width, depth), jnp.bfloat16),
             pltpu.VMEM((CHUNKS, block, depth), jnp.float32),
             pltpu.VMEM((CHUNKS, width, rank), jnp.float32),
             pltpu.VMEM((tokens * n_f, rank), jnp.bfloat16),
             pltpu.VMEM((tokens, depth), jnp.bfloat16),
-            pltpu.VMEM((CHUNKS, half + PAD, rank), jnp.int16),
-            pltpu.VMEM((CHUNKS, half + PAD, rank), jnp.int16),
-            pltpu.VMEM((CHUNKS, n_z - 1, block + PAD, rank), jnp.int16),
-            pltpu.VMEM((CHUNKS, n_z - 1, block + PAD, rank), jnp.int16),
+            pltpu.VMEM((CHUNKS, coded * half + PAD, LANES), jnp.int16),
+            pltpu.VMEM((CHUNKS, coded * half + PAD, LANES), jnp.int16),
+            pltpu.VMEM((CHUNKS, n_z - 1, coded * block + PAD, LANES), jnp.int16),
+            pltpu.VMEM((CHUNKS, n_z - 1, coded * block + PAD, LANES), jnp.int16),
             dma((CHUNKS, n_f - 1)),
             dma((CHUNKS, n_f - 1)),
             dma((n_f - 1,)),
@@ -298,28 +349,24 @@
             dma((4, CHUNKS)),
         ],
         compiler_params=pltpu.CompilerParams(
-            collective_id=0, has_side_effects=True, vmem_limit_bytes=40 * 1024 * 1024
+            collective_id=0, has_side_effects=True, vmem_limit_bytes=52844 * 1024
         ),
         name="mean",
     )(key, act, grads, local, anchor)
 
-    def tile(i):
-        return (i, 0)
-
     return pl.pallas_call(
         update_kernel,
-        grid=(CHUNKS * n_y,),
         out_shape=(
             jax.ShapeDtypeStruct(anchor.shape, anchor.dtype),
             jax.ShapeDtypeStruct(momentum.shape, momentum.dtype),
         ),
-        in_specs=[
-            pl.BlockSpec((1, 1, n_z, block + PAD, rank), lambda i: (i // n_y, i % n_y, 0, 0, 0)),
-            pl.BlockSpec((depth, 2 * rank), lambda i: (0, 0)),
-            pl.BlockSpec((half, depth), tile),
-            pl.BlockSpec((half, rank), tile),
+        in_specs=[vmem] * 4,
+        out_specs=(hbm, hbm),
+        scratch_shapes=[
+            pltpu.VMEM((2, width, depth), jnp.float32),
+            pltpu.VMEM((2, width, rank), jnp.float32),
+            dma((2, 2)),
         ],
-        out_specs=(pl.BlockSpec((half, depth), tile), pl.BlockSpec((half, rank), tile)),
         compiler_params=pltpu.CompilerParams(vmem_limit_bytes=32 * 1024 * 1024),
         name="update",
     )(gathered, proj, anchor, momentum)

time: 71.6 us -> 68.8 us (0.961)
  the two profiles are of different devices: /device:TPU:11 before, /device:TPU:0 now
where the time goes in v2:
time: 68.8 us; the launch traced here: 68.7 us
  Pallas kernels  65 us (94%)
  local copies, waits for them, and re-layouts  3.02 us (4%)
    pallas_call x1, Pallas kernels, in_kernels(): pl.pallas_call(functools.partial(mean_kernel, n_rep, n_y, n_f), out_shape...  58.8 us
    pallas_call x1, Pallas kernels, in_kernels(): pl.pallas_call(update_kernel, out_shape=(jax.ShapeDtypeStruct(anchor.shap...  6.12 us
    unnamed x10, local copies, waits for them, and re-layouts  3.02 us

profile of v2, /device:TPU:0, one launch (start us, length us, event | category | flops | bytes accessed | tf_op | source)
XLA Modules:
  0.0 68.7 jit_solution(3972905975454250201)
XLA Ops:
  0.6 0.0 copy-start.1
  0.6 0.0 copy-start.3
  0.7 1.1 %copy-done.3 = bf16[1,128,1024]{2,1,0:T(8,128)(2,1)S(1)} copy-done((bf16[1,128,1024]{2,1,0:T(8,128)(2,1)S(1)}, bf16[1,128,1024]{2,1,0:T(8,128)(2,1)}, u32[]{:S(2)}) %copy-start.3) | copy-done | bytes 262168
  1.7 0.0 copy-start.4
  1.7 0.7 copy-done.4
  2.4 0.0 copy-start
  2.4 58.8 %mean.1 = (s16[4,2,4,144,128]{4,3,2,1,0:T(8,128)(2,1)}, bf16[1024,512]{1,0:T(8,128)(2,1)S(1)}) custom-call(s32[2]{0:T(128)S(1)} %copy-done.4, bf16[1,128,8192]{2,1,0:T(8,128)(2,1)} %act.1, bf16[1,128,1024]{2,1,0:T(8,128)(2,1)S(1)} %copy-done.3, bf16[1,2048,1024]{2,1,0:T(8,128)(2,1)} %local.1, f32[2048,1024]{1,0:T(8,128)} %anchor.3), custom_call_target="tpu_custom_call" | custom-call | tf_op jit(solution)/shard_map/mean/pallas_call | solution.py:317
  61.2 0.0 copy-done.1
  61.3 0.0 copy-done
  61.3 0.0 copy-start.2
  61.3 1.3 %copy-done.2 = s16[4,2,4,144,128]{4,3,2,1,0:T(8,128)(2,1)S(1)} copy-done((s16[4,2,4,144,128]{4,3,2,1,0:T(8,128)(2,1)S(1)}, s16[4,2,4,144,128]{4,3,2,1,0:T(8,128)(2,1)}, u32[]{:S(2)}) %copy-start.2) | copy-done | bytes 1179672
  62.5 6.1 %update.1 = (f32[2048,1024]{1,0:T(8,128)}, f32[2048,256]{1,0:T(8,128)}) custom-call(s16[4,2,4,144,128]{4,3,2,1,0:T(8,128)(2,1)S(1)} %copy-done.2, bf16[1024,512]{1,0:T(8,128)(2,1)S(1)} %get-tuple-element.5.proj, f32[2048,1024]{1,0:T(8,128)S(1)} %copy-done, f32[2048,256]{1,0:T(8,128)S(1)} %copy-done.1), custom_call_target="tpu_custom_call" | custom-call | tf_op jit(solution)/shard_map/update/pallas_call | solution.py:357
Async XLA Ops:
  0.6 60.6 %copy-start.1 = (f32[2048,256]{1,0:T(8,128)S(1)}, f32[2048,256]{1,0:T(8,128)}, u32[]{:S(2)}) copy-start(f32[2048,256]{1,0:T(8,128)} %momentum.1) | copy-start | bytes 6291460
  0.6 1.1 %copy-start.3 = (bf16[1,128,1024]{2,1,0:T(8,128)(2,1)S(1)}, bf16[1,128,1024]{2,1,0:T(8,128)(2,1)}, u32[]{:S(2)}) copy-start(bf16[1,128,1024]{2,1,0:T(8,128)(2,1)} %grads.1) | copy-start | bytes 786436
  1.7 0.7 copy-start.4
  2.4 58.9 %copy-start = (f32[2048,1024]{1,0:T(8,128)S(1)}, f32[2048,1024]{1,0:T(8,128)}, u32[]{:S(2)}) copy-start(f32[2048,1024]{1,0:T(8,128)} %anchor.3) | copy-start | bytes 25165828
  61.3 1.3 %copy-start.2 = (s16[4,2,4,144,128]{4,3,2,1,0:T(8,128)(2,1)S(1)}, s16[4,2,4,144,128]{4,3,2,1,0:T(8,128)(2,1)}, u32[]{:S(2)}) copy-start(s16[4,2,4,144,128]{4,3,2,1,0:T(8,128)(2,1)} %get-tuple-element.4.gathered) | copy-start | bytes 3538948

commit v3 on v2

--- a/solution.py
+++ b/solution.py
@@ -9,18 +9,20 @@
 
 HIGH = lax.Precision.HIGHEST
 MESH = pl.DeviceIdType.MESH
-CHUNKS = 4
+CHUNKS = 8
+AHEAD = 3
+GROUP = 2
 PAD = 16
 LANES = 128
 LEVELS = 32500.0
 STEPS = 256.0
-NT = (((1,), (1,)), ((), ()))
 TN = (((0,), (0,)), ((), ()))
 
 
-def projection(word0, word1, rows, cols, first=0):
-    k_index = lax.broadcasted_iota(jnp.int32, (rows, cols), 0) + first
-    r_index = lax.broadcasted_iota(jnp.int32, (rows, cols), 1)
+def projection(word0, word1, rows, cols, first=0, turned=False):
+    shape = (cols, rows) if turned else (rows, cols)
+    k_index = lax.broadcasted_iota(jnp.int32, shape, int(turned)) + first
+    r_index = lax.broadcasted_iota(jnp.int32, shape, int(not turned))
     hashed = word0 + k_index * 668265261 + r_index * 374761393 + word1 * 1103515245
     hashed = jnp.bitwise_xor(hashed, lax.shift_right_logical(hashed, jnp.int32(15)))
     hashed = hashed * 739982445
@@ -73,8 +75,8 @@
 
 
 def mean_kernel(
-    n_rep, n_y, n_f, key_hbm, act, grads, local, anchor, gathered, proj,
-    key, columns, weights, own_anchor, total, pg, grads_in, y_out, y_in, z_out, z_in,
+    n_rep, n_y, n_f, key_hbm, act, grads, local, anchor, gathered, turned,
+    key, proj, columns, weights, own_anchor, total, pg, grads_in, y_out, y_in, z_out, z_in,
     act_s, act_r, pg_s, pg_r, y1_s, y1_r, z1_s, z1_r, z2_s, z2_r, y2_s, y2_r, here,
 ):
     n_z = n_rep // n_y
@@ -176,17 +178,21 @@
     pg[mine, :] = (both[:, :rank] + both[:, rank:]).astype(jnp.bfloat16)
     for d in order:
         pg_copy(d).start()
-    for d in order:
-        act_copy(1, d).start()
+    for c in range(1, min(AHEAD, chunks)):
+        for d in order:
+            act_copy(c, d).start()
 
     @pl.loop(0, chunks)
     def _(c):
         weight_copy(c).wait()
-        for h in range(n_y):
-            at = pl.ds(h * half, half)
-            both = dot(weights[c, at, :], proj[...])
-            total[c, at, :] = (both[:, :rank] + both[:, rank:]) * (-1.0 / n_rep)
-
+        both = dot(weights[c], proj[...])
+        total[c] = (both[:, :rank] + both[:, rank:]) * (-1.0 / n_rep)
+
+    for k in range(0, depth, rank):
+        high, low = split(projection(key[0], key[1], rank, rank, k, True))
+        turned[:rank, k : k + rank] = high
+        turned[rank : 2 * rank, k : k + rank] = low
+        turned[2 * rank :, k : k + rank] = high
     for d in range(1, n_f):
         pg_copy(d).wait_recv()
     scale = float(tokens_all) ** (-0.5) / n_rep
@@ -196,10 +202,10 @@
         for d in range(1, n_f):
             act_copy(c, d).wait_recv()
 
-        @pl.when(c + 2 < chunks)
+        @pl.when(c + AHEAD < chunks)
         def _():
             for d in order:
-                act_copy(c + 2, d).start()
+                act_copy(c + AHEAD, d).start()
 
         total[c] += dot(columns[c], pg[...], TN) * scale
         far = pl.ds(pl.multiple_of(other * half, half), half)
@@ -234,9 +240,9 @@
             z2_copy(c, d).wait_recv()
         y2_copy(c).start()
 
-    stages = ((partial_sum, 0), (hand_over, 2), (whole_mean, 1), (sum_of_pair, 0))
-
-    @pl.loop(0, chunks + 2)
+    stages = ((partial_sum, 0), (hand_over, 4), (sum_of_pair, 1), (whole_mean, 2))
+
+    @pl.loop(0, chunks + 4)
     def _(t):
         for stage, lag in stages:
 
@@ -260,12 +266,12 @@
 
 
 def update_kernel(
-    gathered, proj, anchor, momentum, new_anchor, new_momentum, anchor_out, momentum_out, sems
+    gathered, turned, anchor, momentum, new_anchor, new_momentum, anchor_out, momentum_out, sems
 ):
     chunks, n_y, n_z = gathered.shape[:3]
     rank = momentum.shape[1]
-    width = momentum.shape[0] // chunks
-    block = width // n_y // n_z
+    steps = chunks // GROUP
+    width = momentum.shape[0] // steps
 
     def stores(c):
         at = pl.ds(pl.multiple_of(c * width, width), width)
@@ -275,7 +281,7 @@
             pltpu.make_async_copy(momentum_out.at[slot], new_momentum.at[at, :], sems.at[1, slot]),
         )
 
-    @pl.loop(0, chunks)
+    @pl.loop(0, steps)
     def _(c):
         slot = c % 2
 
@@ -285,19 +291,24 @@
                 store.wait()
 
         mean = jnp.concatenate(
-            [decode(gathered.at[c, h, q], rank) for h in range(n_y) for q in range(n_z)], axis=0
+            [
+                decode(gathered.at[c * GROUP + g, h, q], rank)
+                for g in range(GROUP)
+                for h in range(n_y)
+                for q in range(n_z)
+            ],
+            axis=0,
         )
         at = pl.ds(pl.multiple_of(c * width, width), width)
         moved = 0.9 * momentum[at, :] + mean
         momentum_out[slot] = moved
         high, low = split(mean + 0.9 * moved)
-        step = dot(jnp.concatenate([high, high], axis=1), proj[...], NT)
-        step += dot(low, proj[:, :rank], NT)
+        step = dot(jnp.concatenate([high, high, low], axis=1), turned[...])
         anchor_out[slot] = anchor[at, :] - 0.7 * step
         for store in stores(c):
             store.start()
 
-    for c in range(max(chunks - 2, 0), chunks):
+    for c in range(max(steps - 2, 0), steps):
         for store in stores(c):
             store.wait()
 
@@ -314,16 +325,17 @@
     hbm = pl.BlockSpec(memory_space=pltpu.HBM)
     coded = rank // LANES
     vmem = pl.BlockSpec(memory_space=pltpu.VMEM)
-    gathered, proj = pl.pallas_call(
+    gathered, turned = pl.pallas_call(
         functools.partial(mean_kernel, n_rep, n_y, n_f),
         out_shape=(
             jax.ShapeDtypeStruct((CHUNKS, n_y, n_z, coded * block + PAD, LANES), jnp.int16),
-            jax.ShapeDtypeStruct((depth, 2 * rank), jnp.bfloat16),
+            jax.ShapeDtypeStruct((3 * rank, depth), jnp.bfloat16),
         ),
         in_specs=[hbm] * 5,
         out_specs=(vmem, vmem),
         scratch_shapes=[
             pltpu.SMEM(key.shape, jnp.int32),
+            pltpu.VMEM((depth, 2 * rank), jnp.bfloat16),
             pltpu.VMEM((CHUNKS, tokens * n_f, width), jnp.bfloat16),
             pltpu.VMEM((CHUNKS, width, depth), jnp.bfloat16),
             pltpu.VMEM((CHUNKS, block, depth), jnp.float32),
@@ -349,7 +361,7 @@
             dma((4, CHUNKS)),
         ],
         compiler_params=pltpu.CompilerParams(
-            collective_id=0, has_side_effects=True, vmem_limit_bytes=52844 * 1024
+            collective_id=0, has_side_effects=True, vmem_limit_bytes=51700 * 1024
         ),
         name="mean",
     )(key, act, grads, local, anchor)
@@ -363,13 +375,13 @@
         in_specs=[vmem] * 4,
         out_specs=(hbm, hbm),
         scratch_shapes=[
-            pltpu.VMEM((2, width, depth), jnp.float32),
-            pltpu.VMEM((2, width, rank), jnp.float32),
+            pltpu.VMEM((2, GROUP * width, depth), jnp.float32),
+            pltpu.VMEM((2, GROUP * width, rank), jnp.float32),
             dma((2, 2)),
         ],
         compiler_params=pltpu.CompilerParams(vmem_limit_bytes=32 * 1024 * 1024),
         name="update",
-    )(gathered, proj, anchor, momentum)
+    )(gathered, turned, anchor, momentum)
 
 
 def in_steps(activations, grad_out, local_weight, anchor, momentum, projection_key):

time: 68.8 us -> 63.6 us (0.924)
  Pallas kernels: 65 us -> 61 us
  local copies, waits for them, and re-layouts: 3.02 us -> 1.75 us
    pallas_call x1, Pallas kernels: 58.8 us -> 54.9 us  [in_kernels(): pl.pallas_call(functools.partial(mean_kernel, n_rep, n_y, n_f), out_shape...]
    unnamed x10 -> x8, local copies, waits for them, and re-layouts: 3.02 us -> 1.75 us
where the time goes in v3:
time: 63.6 us; the launch traced here: 63.5 us
  Pallas kernels  61 us (96%)
  local copies, waits for them, and re-layouts  1.75 us (3%)
  between operations  0.67 us (1%)
    pallas_call x1, Pallas kernels, in_kernels(): pl.pallas_call(functools.partial(mean_kernel, n_rep, n_y, n_f), out_shape...  54.9 us
    pallas_call x1, Pallas kernels, in_kernels(): pl.pallas_call(update_kernel, out_shape=(jax.ShapeDtypeStruct(anchor.shap...  6.12 us
    unnamed x8, local copies, waits for them, and re-layouts  1.75 us

profile of v3, /device:TPU:0, one launch (start us, length us, event | category | flops | bytes accessed | tf_op | source)
XLA Modules:
  0.0 63.5 jit_solution(13402776397248645576)
XLA Ops:
  0.6 0.0 copy-start.1
  0.6 0.0 copy-start.2
  0.7 1.1 %copy-done.2 = bf16[1,128,1024]{2,1,0:T(8,128)(2,1)S(1)} copy-done((bf16[1,128,1024]{2,1,0:T(8,128)(2,1)S(1)}, bf16[1,128,1024]{2,1,0:T(8,128)(2,1)}, u32[]{:S(2)}) %copy-start.2) | copy-done | bytes 262168
  1.7 0.0 copy-start.3
  1.7 0.7 %copy-done.3 = s32[2]{0:T(128)S(1)} copy-done((s32[2]{0:T(128)S(1)}, s32[2]{0:T(128)}, u32[]{:S(2)}) %copy-start.3) | copy-done | bytes 32
  2.4 0.0 copy-start
  2.4 54.9 %mean.1 = (s16[8,2,4,80,128]{4,3,2,1,0:T(8,128)(2,1)S(1)}, bf16[768,1024]{1,0:T(8,128)(2,1)S(1)}) custom-call(s32[2]{0:T(128)S(1)} %copy-done.3, bf16[1,128,8192]{2,1,0:T(8,128)(2,1)} %act.1, bf16[1,128,1024]{2,1,0:T(8,128)(2,1)S(1)} %copy-done.2, bf16[1,2048,1024]{2,1,0:T(8,128)(2,1)} %local.1, f32[2048,1024]{1,0:T(8,128)} %anchor.3), custom_call_target="tpu_custom_call" | custom-call | tf_op jit(solution)/shard_map/mean/pallas_call | solution.py:328
  57.3 0.0 copy-done.1
  57.3 0.0 copy-done
  57.3 6.1 %update.1 = (f32[2048,1024]{1,0:T(8,128)}, f32[2048,256]{1,0:T(8,128)}) custom-call(s16[8,2,4,80,128]{4,3,2,1,0:T(8,128)(2,1)S(1)} %get-tuple-element.4.gathered, bf16[768,1024]{1,0:T(8,128)(2,1)S(1)} %get-tuple-element.5.turned, f32[2048,1024]{1,0:T(8,128)S(1)} %copy-done, f32[2048,256]{1,0:T(8,128)S(1)} %copy-done.1), custom_call_target="tpu_custom_call" | custom-call | tf_op jit(solution)/shard_map/update/pallas_call | solution.py:369
Async XLA Ops:
  0.6 56.7 %copy-start.1 = (f32[2048,256]{1,0:T(8,128)S(1)}, f32[2048,256]{1,0:T(8,128)}, u32[]{:S(2)}) copy-start(f32[2048,256]{1,0:T(8,128)} %momentum.1) | copy-start | bytes 6291460
  0.6 1.1 %copy-start.2 = (bf16[1,128,1024]{2,1,0:T(8,128)(2,1)S(1)}, bf16[1,128,1024]{2,1,0:T(8,128)(2,1)}, u32[]{:S(2)}) copy-start(bf16[1,128,1024]{2,1,0:T(8,128)(2,1)} %grads.1) | copy-start | bytes 786436
  1.7 0.7 %copy-start.3 = (s32[2]{0:T(128)S(1)}, s32[2]{0:T(128)}, u32[]{:S(2)}) copy-start(s32[2]{0:T(128)} %key_hbm.1) | copy-start | bytes 28
  2.4 54.9 %copy-start = (f32[2048,1024]{1,0:T(8,128)S(1)}, f32[2048,1024]{1,0:T(8,128)}, u32[]{:S(2)}) copy-start(f32[2048,1024]{1,0:T(8,128)} %anchor.3) | copy-start | bytes 25165828

commit v4 on v3

--- a/solution.py
+++ b/solution.py
@@ -44,19 +44,24 @@
     return lax.dot_general(a, b, dims, preferred_element_type=jnp.float32)
 
 
-def encode(value, ref):
-    rows, cols = value.shape
+def encode(value, refs):
+    cols = value.shape[1]
+    parts, rows = cols // LANES, value.shape[0] // len(refs)
     top = jnp.max(jnp.abs(value), axis=0, keepdims=True)
     power = jnp.ceil(jnp.log(jnp.maximum(top, 1e-30)) * (STEPS * 1.4426950408889634))
     factor = jnp.exp2(power * (-1.0 / STEPS)) * LEVELS
     coded = jnp.round(value * factor).astype(jnp.int32).astype(jnp.int16)
     line = lax.broadcasted_iota(jnp.int32, (PAD, LANES), 0)
     scales = jnp.zeros((PAD, LANES), jnp.float32)
-    for part in range(cols // LANES):
-        at = slice(part * LANES, (part + 1) * LANES)
-        ref[part * rows : (part + 1) * rows, :] = coded[:, at]
-        scales = jnp.where(line == part, power[:, at], scales)
-    ref[cols // LANES * rows :, :] = scales.astype(jnp.int32).astype(jnp.int16)
+    for part in range(parts):
+        scales = jnp.where(line == part, power[:, part * LANES : (part + 1) * LANES], scales)
+    scales = scales.astype(jnp.int32).astype(jnp.int16)
+    for n, ref in enumerate(refs):
+        for part in range(parts):
+            ref[part * rows : (part + 1) * rows, :] = coded[
+                n * rows : (n + 1) * rows, part * LANES : (part + 1) * LANES
+            ]
+        ref[parts * rows :, :] = scales
 
 
 def decode(ref, cols):
@@ -76,7 +81,7 @@
 
 def mean_kernel(
     n_rep, n_y, n_f, key_hbm, act, grads, local, anchor, gathered, turned,
-    key, proj, columns, weights, own_anchor, total, pg, grads_in, y_out, y_in, z_out, z_in,
+    key, proj, columns, weights, own_anchor, base, total, pg, grads_in, y_out, y_in, z_out, z_in,
     act_s, act_r, pg_s, pg_r, y1_s, y1_r, z1_s, z1_r, z2_s, z2_r, y2_s, y2_r, here,
 ):
     n_z = n_rep // n_y
@@ -128,7 +133,7 @@
 
     def anchor_copy(c):
         at = pl.ds(pl.multiple_of(c * width + y * half + z * block, block), block)
-        return pltpu.make_async_copy(anchor.at[at, :], own_anchor.at[c], here.at[2, c])
+        return pltpu.make_async_copy(anchor.at[at, :], own_anchor.at[pl.ds(c * block, block), :], here.at[2, c])
 
     def pg_copy(d):
         return remote(
@@ -140,7 +145,7 @@
 
     def z1_copy(c, d):
         return remote(
-            z_out.at[c, d - 1], z_in.at[c, d - 1], z1_s.at[c, d - 1], z1_r.at[c, d - 1], z_peer(d)
+            z_out.at[c, (z + d) % n_z], z_in.at[c, d - 1], z1_s.at[c, d - 1], z1_r.at[c, d - 1], z_peer(d)
         )
 
     def z2_copy(c, d):
@@ -188,6 +193,12 @@
         both = dot(weights[c], proj[...])
         total[c] = (both[:, :rank] + both[:, rank:]) * (-1.0 / n_rep)
 
+    for c in range(chunks):
+        anchor_copy(c).wait()
+    high, low = split(own_anchor[...])
+    both = dot(high, proj[...])
+    base[...] = both[:, :rank] + both[:, rank:] + dot(low, proj[:, :rank])
+
     for k in range(0, depth, rank):
         high, low = split(projection(key[0], key[1], rank, rank, k, True))
         turned[:rank, k : k + rank] = high
@@ -209,29 +220,26 @@
 
         total[c] += dot(columns[c], pg[...], TN) * scale
         far = pl.ds(pl.multiple_of(other * half, half), half)
-        encode(total[c, far, :], y_out.at[c])
+        encode(total[c, far, :], [y_out.at[c]])
         y1_copy(c).start()
 
     def sum_of_pair(c):
         y1_copy(c).wait_recv()
         near = pl.ds(pl.multiple_of(y * half, half), half)
-        total[c, near, :] += decode(y_in.at[c], rank)
+        pair = total[c, near, :] + decode(y_in.at[c], rank)
+        total[c, near, :] = pair
+        encode(pair, [z_out.at[c, q] for q in range(n_z)])
         for d in range(1, n_z):
-            q = (z + d) % n_z
-            at = pl.ds(pl.multiple_of(y * half + q * block, block), block)
-            encode(total[c, at, :], z_out.at[c, d - 1])
             z1_copy(c, d).start()
 
     def whole_mean(c):
         at = pl.ds(pl.multiple_of(y * half + z * block, block), block)
-        anchor_copy(c).wait()
-        high, low = split(own_anchor[c])
-        both = dot(high, proj[...])
-        value = total[c, at, :] + both[:, :rank] + both[:, rank:] + dot(low, proj[:, :rank])
+        own = pl.ds(pl.multiple_of(c * block, block), block)
+        value = total[c, at, :] + base[own, :]
         for d in range(1, n_z):
             z1_copy(c, d).wait_recv()
             value += decode(z_in.at[c, d - 1], rank)
-        encode(value, gathered.at[c, y, z])
+        encode(value, [gathered.at[c, y, z]])
         for d in range(1, n_z):
             z2_copy(c, d).start()
 
@@ -338,13 +346,14 @@
             pltpu.VMEM((depth, 2 * rank), jnp.bfloat16),
             pltpu.VMEM((CHUNKS, tokens * n_f, width), jnp.bfloat16),
             pltpu.VMEM((CHUNKS, width, depth), jnp.bfloat16),
-            pltpu.VMEM((CHUNKS, block, depth), jnp.float32),
+            pltpu.VMEM((CHUNKS * block, depth), jnp.float32),
+            pltpu.VMEM((CHUNKS * block, rank), jnp.float32),
             pltpu.VMEM((CHUNKS, width, rank), jnp.float32),
             pltpu.VMEM((tokens * n_f, rank), jnp.bfloat16),
             pltpu.VMEM((tokens, depth), jnp.bfloat16),
             pltpu.VMEM((CHUNKS, coded * half + PAD, LANES), jnp.int16),
             pltpu.VMEM((CHUNKS, coded * half + PAD, LANES), jnp.int16),
-            pltpu.VMEM((CHUNKS, n_z - 1, coded * block + PAD, LANES), jnp.int16),
+            pltpu.VMEM((CHUNKS, n_z, coded * block + PAD, LANES), jnp.int16),
             pltpu.VMEM((CHUNKS, n_z - 1, coded * block + PAD, LANES), jnp.int16),
             dma((CHUNKS, n_f - 1)),
             dma((CHUNKS, n_f - 1)),

time: 63.6 us -> 63.6 us (level)
  no operation moved by 1% of the time
where the time goes in v4:
time: 63.6 us; the launch traced here: 63.5 us
  Pallas kernels  61 us (96%)
  local copies, waits for them, and re-layouts  1.75 us (3%)
  between operations  0.67 us (1%)
    pallas_call x1, Pallas kernels, in_kernels(): pl.pallas_call(functools.partial(mean_kernel, n_rep, n_y, n_f), out_shape...  54.9 us
    pallas_call x1, Pallas kernels, in_kernels(): pl.pallas_call(update_kernel, out_shape=(jax.ShapeDtypeStruct(anchor.shap...  6.11 us
    unnamed x8, local copies, waits for them, and re-layouts  1.75 us

profile of v4, /device:TPU:0, one launch (start us, length us, event | category | flops | bytes accessed | tf_op | source)
XLA Modules:
  0.0 63.5 jit_solution(2349122100472600498)
XLA Ops:
  0.6 0.0 copy-start.1
  0.6 0.0 copy-start.2
  0.7 1.1 %copy-done.2 = bf16[1,128,1024]{2,1,0:T(8,128)(2,1)S(1)} copy-done((bf16[1,128,1024]{2,1,0:T(8,128)(2,1)S(1)}, bf16[1,128,1024]{2,1,0:T(8,128)(2,1)}, u32[]{:S(2)}) %copy-start.2) | copy-done | bytes 262168
  1.7 0.0 copy-start.3
  1.7 0.7 %copy-done.3 = s32[2]{0:T(128)S(1)} copy-done((s32[2]{0:T(128)S(1)}, s32[2]{0:T(128)}, u32[]{:S(2)}) %copy-start.3) | copy-done | bytes 32
  2.4 0.0 copy-start
  2.4 54.9 %mean.1 = (s16[8,2,4,80,128]{4,3,2,1,0:T(8,128)(2,1)S(1)}, bf16[768,1024]{1,0:T(8,128)(2,1)S(1)}) custom-call(s32[2]{0:T(128)S(1)} %copy-done.3, bf16[1,128,8192]{2,1,0:T(8,128)(2,1)} %act.1, bf16[1,128,1024]{2,1,0:T(8,128)(2,1)S(1)} %copy-done.2, bf16[1,2048,1024]{2,1,0:T(8,128)(2,1)} %local.1, f32[2048,1024]{1,0:T(8,128)} %anchor.3), custom_call_target="tpu_custom_call" | custom-call | tf_op jit(solution)/shard_map/mean/pallas_call | solution.py:336
  57.3 0.0 copy-done.1
  57.3 0.0 copy-done
  57.3 6.1 %update.1 = (f32[2048,1024]{1,0:T(8,128)}, f32[2048,256]{1,0:T(8,128)}) custom-call(s16[8,2,4,80,128]{4,3,2,1,0:T(8,128)(2,1)S(1)} %get-tuple-element.4.gathered, bf16[768,1024]{1,0:T(8,128)(2,1)S(1)} %get-tuple-element.5.turned, f32[2048,1024]{1,0:T(8,128)S(1)} %copy-done, f32[2048,256]{1,0:T(8,128)S(1)} %copy-done.1), custom_call_target="tpu_custom_call" | custom-call | tf_op jit(solution)/shard_map/update/pallas_call | solution.py:378
Async XLA Ops:
  0.6 56.7 %copy-start.1 = (f32[2048,256]{1,0:T(8,128)S(1)}, f32[2048,256]{1,0:T(8,128)}, u32[]{:S(2)}) copy-start(f32[2048,256]{1,0:T(8,128)} %momentum.1) | copy-start | bytes 6291460
  0.6 1.1 %copy-start.2 = (bf16[1,128,1024]{2,1,0:T(8,128)(2,1)S(1)}, bf16[1,128,1024]{2,1,0:T(8,128)(2,1)}, u32[]{:S(2)}) copy-start(bf16[1,128,1024]{2,1,0:T(8,128)(2,1)} %grads.1) | copy-start | bytes 786436
  1.7 0.7 %copy-start.3 = (s32[2]{0:T(128)S(1)}, s32[2]{0:T(128)}, u32[]{:S(2)}) copy-start(s32[2]{0:T(128)} %key_hbm.1) | copy-start | bytes 28
  2.4 54.9 %copy-start = (f32[2048,1024]{1,0:T(8,128)S(1)}, f32[2048,1024]{1,0:T(8,128)}, u32[]{:S(2)}) copy-start(f32[2048,1024]{1,0:T(8,128)} %anchor.3) | copy-start | bytes 25165828

commit v5 on v4

--- a/solution.py
+++ b/solution.py
@@ -10,7 +10,7 @@
 HIGH = lax.Precision.HIGHEST
 MESH = pl.DeviceIdType.MESH
 CHUNKS = 8
-AHEAD = 3
+AHEAD = 4
 GROUP = 2
 PAD = 16
 LANES = 128
@@ -248,9 +248,9 @@
             z2_copy(c, d).wait_recv()
         y2_copy(c).start()
 
-    stages = ((partial_sum, 0), (hand_over, 4), (sum_of_pair, 1), (whole_mean, 2))
-
-    @pl.loop(0, chunks + 4)
+    stages = ((partial_sum, 0), (hand_over, 6), (whole_mean, 4), (sum_of_pair, 2))
+
+    @pl.loop(0, chunks + 6)
     def _(t):
         for stage, lag in stages:
 

time: 63.6 us -> 66.9 us (1.052)
  Pallas kernels: 61 us -> 64.3 us
    pallas_call x1, Pallas kernels: 54.9 us -> 58.2 us  [in_kernels(): pl.pallas_call(functools.partial(mean_kernel, n_rep, n_y, n_f), out_shape...]
where the time goes in v5:
time: 66.9 us; the launch traced here: 66.7 us
  Pallas kernels  64.3 us (96%)
  local copies, waits for them, and re-layouts  1.75 us (3%)
  between operations  0.67 us (1%)
    pallas_call x1, Pallas kernels, in_kernels(): pl.pallas_call(functools.partial(mean_kernel, n_rep, n_y, n_f), out_shape...  58.2 us
    pallas_call x1, Pallas kernels, in_kernels(): pl.pallas_call(update_kernel, out_shape=(jax.ShapeDtypeStruct(anchor.shap...  6.12 us
    unnamed x8, local copies, waits for them, and re-layouts  1.75 us

profile of v5, /device:TPU:0, one launch (start us, length us, event | category | flops | bytes accessed | tf_op | source)
XLA Modules:
  0.0 66.7 jit_solution(14805216885328064341)
XLA Ops:
  0.6 0.0 copy-start.1
  0.6 0.0 copy-start.2
  0.7 1.1 %copy-done.2 = bf16[1,128,1024]{2,1,0:T(8,128)(2,1)S(1)} copy-done((bf16[1,128,1024]{2,1,0:T(8,128)(2,1)S(1)}, bf16[1,128,1024]{2,1,0:T(8,128)(2,1)}, u32[]{:S(2)}) %copy-start.2) | copy-done | bytes 262168
  1.7 0.0 copy-start.3
  1.7 0.7 copy-done.3
  2.4 0.0 copy-start
  2.4 58.2 %mean.1 = (s16[8,2,4,80,128]{4,3,2,1,0:T(8,128)(2,1)S(1)}, bf16[768,1024]{1,0:T(8,128)(2,1)S(1)}) custom-call(s32[2]{0:T(128)S(1)} %copy-done.3, bf16[1,128,8192]{2,1,0:T(8,128)(2,1)} %act.1, bf16[1,128,1024]{2,1,0:T(8,128)(2,1)S(1)} %copy-done.2, bf16[1,2048,1024]{2,1,0:T(8,128)(2,1)} %local.1, f32[2048,1024]{1,0:T(8,128)} %anchor.3), custom_call_target="tpu_custom_call" | custom-call | tf_op jit(solution)/shard_map/mean/pallas_call | solution.py:336
  60.6 0.0 copy-done.1
  60.6 0.0 copy-done
  60.6 6.1 %update.1 = (f32[2048,1024]{1,0:T(8,128)}, f32[2048,256]{1,0:T(8,128)}) custom-call(s16[8,2,4,80,128]{4,3,2,1,0:T(8,128)(2,1)S(1)} %get-tuple-element.4.gathered, bf16[768,1024]{1,0:T(8,128)(2,1)S(1)} %get-tuple-element.5.turned, f32[2048,1024]{1,0:T(8,128)S(1)} %copy-done, f32[2048,256]{1,0:T(8,128)S(1)} %copy-done.1), custom_call_target="tpu_custom_call" | custom-call | tf_op jit(solution)/shard_map/update/pallas_call | solution.py:378
Async XLA Ops:
  0.6 60.0 %copy-start.1 = (f32[2048,256]{1,0:T(8,128)S(1)}, f32[2048,256]{1,0:T(8,128)}, u32[]{:S(2)}) copy-start(f32[2048,256]{1,0:T(8,128)} %momentum.1) | copy-start | bytes 6291460
  0.6 1.1 %copy-start.2 = (bf16[1,128,1024]{2,1,0:T(8,128)(2,1)S(1)}, bf16[1,128,1024]{2,1,0:T(8,128)(2,1)}, u32[]{:S(2)}) copy-start(bf16[1,128,1024]{2,1,0:T(8,128)(2,1)} %grads.1) | copy-start | bytes 786436
  1.7 0.7 copy-start.3
  2.4 58.2 %copy-start = (f32[2048,1024]{1,0:T(8,128)S(1)}, f32[2048,1024]{1,0:T(8,128)}, u32[]{:S(2)}) copy-start(f32[2048,1024]{1,0:T(8,128)} %anchor.3) | copy-start | bytes 25165828

commit v6 on v4

--- a/solution.py
+++ b/solution.py
@@ -248,9 +248,9 @@
             z2_copy(c, d).wait_recv()
         y2_copy(c).start()
 
-    stages = ((partial_sum, 0), (hand_over, 4), (sum_of_pair, 1), (whole_mean, 2))
-
-    @pl.loop(0, chunks + 4)
+    stages = ((partial_sum, 0), (hand_over, 2), (whole_mean, 1), (sum_of_pair, 0))
+
+    @pl.loop(0, chunks + 2)
     def _(t):
         for stage, lag in stages:
 

time: 63.6 us -> 73.9 us (1.16)
  Pallas kernels: 61 us -> 71.3 us
    pallas_call x1, Pallas kernels: 54.9 us -> 65.2 us  [in_kernels(): pl.pallas_call(functools.partial(mean_kernel, n_rep, n_y, n_f), out_shape...]
where the time goes in v6:
time: 73.9 us; the launch traced here: 73.7 us
  Pallas kernels  71.3 us (96%)
  local copies, waits for them, and re-layouts  1.75 us (2%)
    pallas_call x1, Pallas kernels, in_kernels(): pl.pallas_call(functools.partial(mean_kernel, n_rep, n_y, n_f), out_shape...  65.2 us
    pallas_call x1, Pallas kernels, in_kernels(): pl.pallas_call(update_kernel, out_shape=(jax.ShapeDtypeStruct(anchor.shap...  6.12 us
    unnamed x8, local copies, waits for them, and re-layouts  1.75 us

profile of v6, /device:TPU:0, one launch (start us, length us, event | category | flops | bytes accessed | tf_op | source)
XLA Modules:
  0.0 73.7 jit_solution(17076237740459517537)
XLA Ops:
  0.6 0.0 copy-start.1
  0.6 0.0 copy-start.2
  0.7 1.1 %copy-done.2 = bf16[1,128,1024]{2,1,0:T(8,128)(2,1)S(1)} copy-done((bf16[1,128,1024]{2,1,0:T(8,128)(2,1)S(1)}, bf16[1,128,1024]{2,1,0:T(8,128)(2,1)}, u32[]{:S(2)}) %copy-start.2) | copy-done | bytes 262168
  1.7 0.0 copy-start.3
  1.7 0.7 copy-done.3
  2.4 0.0 copy-start
  2.4 65.2 %mean.1 = (s16[8,2,4,80,128]{4,3,2,1,0:T(8,128)(2,1)S(1)}, bf16[768,1024]{1,0:T(8,128)(2,1)S(1)}) custom-call(s32[2]{0:T(128)S(1)} %copy-done.3, bf16[1,128,8192]{2,1,0:T(8,128)(2,1)} %act.1, bf16[1,128,1024]{2,1,0:T(8,128)(2,1)S(1)} %copy-done.2, bf16[1,2048,1024]{2,1,0:T(8,128)(2,1)} %local.1, f32[2048,1024]{1,0:T(8,128)} %anchor.3), custom_call_target="tpu_custom_call" | custom-call | tf_op jit(solution)/shard_map/mean/pallas_call | solution.py:336
  67.6 0.0 copy-done.1
  67.6 0.0 copy-done
  67.6 6.1 %update.1 = (f32[2048,1024]{1,0:T(8,128)}, f32[2048,256]{1,0:T(8,128)}) custom-call(s16[8,2,4,80,128]{4,3,2,1,0:T(8,128)(2,1)S(1)} %get-tuple-element.4.gathered, bf16[768,1024]{1,0:T(8,128)(2,1)S(1)} %get-tuple-element.5.turned, f32[2048,1024]{1,0:T(8,128)S(1)} %copy-done, f32[2048,256]{1,0:T(8,128)S(1)} %copy-done.1), custom_call_target="tpu_custom_call" | custom-call | tf_op jit(solution)/shard_map/update/pallas_call | solution.py:378
Async XLA Ops:
  0.6 67.0 %copy-start.1 = (f32[2048,256]{1,0:T(8,128)S(1)}, f32[2048,256]{1,0:T(8,128)}, u32[]{:S(2)}) copy-start(f32[2048,256]{1,0:T(8,128)} %momentum.1) | copy-start | bytes 6291460
  0.6 1.1 %copy-start.2 = (bf16[1,128,1024]{2,1,0:T(8,128)(2,1)S(1)}, bf16[1,128,1024]{2,1,0:T(8,128)(2,1)}, u32[]{:S(2)}) copy-start(bf16[1,128,1024]{2,1,0:T(8,128)(2,1)} %grads.1) | copy-start | bytes 786436
  1.7 0.7 copy-start.3
  2.4 65.2 %copy-start = (f32[2048,1024]{1,0:T(8,128)S(1)}, f32[2048,1024]{1,0:T(8,128)}, u32[]{:S(2)}) copy-start(f32[2048,1024]{1,0:T(8,128)} %anchor.3) | copy-start | bytes 25165828

commit v7 on v4

--- a/solution.py
+++ b/solution.py
@@ -10,7 +10,7 @@
 HIGH = lax.Precision.HIGHEST
 MESH = pl.DeviceIdType.MESH
 CHUNKS = 8
-AHEAD = 3
+AHEAD = 2
 GROUP = 2
 PAD = 16
 LANES = 128
@@ -213,15 +213,15 @@
         for d in range(1, n_f):
             act_copy(c, d).wait_recv()
 
+        total[c] += dot(columns[c], pg[...], TN) * scale
+        far = pl.ds(pl.multiple_of(other * half, half), half)
+        encode(total[c, far, :], [y_out.at[c]])
+        y1_copy(c).start()
+
         @pl.when(c + AHEAD < chunks)
         def _():
             for d in order:
                 act_copy(c + AHEAD, d).start()
-
-        total[c] += dot(columns[c], pg[...], TN) * scale
-        far = pl.ds(pl.multiple_of(other * half, half), half)
-        encode(total[c, far, :], [y_out.at[c]])
-        y1_copy(c).start()
 
     def sum_of_pair(c):
         y1_copy(c).wait_recv()

time: 63.6 us -> 63.1 us (level)
  no operation moved by 1% of the time
where the time goes in v7:
time: 63.1 us; the launch traced here: 63 us
  Pallas kernels  60.5 us (96%)
  local copies, waits for them, and re-layouts  1.75 us (3%)
  between operations  0.67 us (1%)
    pallas_call x1, Pallas kernels, in_kernels(): pl.pallas_call(functools.partial(mean_kernel, n_rep, n_y, n_f), out_shape...  54.4 us
    pallas_call x1, Pallas kernels, in_kernels(): pl.pallas_call(update_kernel, out_shape=(jax.ShapeDtypeStruct(anchor.shap...  6.12 us
    unnamed x8, local copies, waits for them, and re-layouts  1.75 us

profile of v7, /device:TPU:0, one launch (start us, length us, event | category | flops | bytes accessed | tf_op | source)
XLA Modules:
  0.0 63.0 jit_solution(15296995650010950138)
XLA Ops:
  0.6 0.0 copy-start.1
  0.6 0.0 copy-start.2
  0.7 1.1 %copy-done.2 = bf16[1,128,1024]{2,1,0:T(8,128)(2,1)S(1)} copy-done((bf16[1,128,1024]{2,1,0:T(8,128)(2,1)S(1)}, bf16[1,128,1024]{2,1,0:T(8,128)(2,1)}, u32[]{:S(2)}) %copy-start.2) | copy-done | bytes 262168
  1.7 0.0 copy-start.3
  1.7 0.7 %copy-done.3 = s32[2]{0:T(128)S(1)} copy-done((s32[2]{0:T(128)S(1)}, s32[2]{0:T(128)}, u32[]{:S(2)}) %copy-start.3) | copy-done | bytes 32
  2.4 0.0 copy-start
  2.4 54.4 %mean.1 = (s16[8,2,4,80,128]{4,3,2,1,0:T(8,128)(2,1)S(1)}, bf16[768,1024]{1,0:T(8,128)(2,1)S(1)}) custom-call(s32[2]{0:T(128)S(1)} %copy-done.3, bf16[1,128,8192]{2,1,0:T(8,128)(2,1)} %act.1, bf16[1,128,1024]{2,1,0:T(8,128)(2,1)S(1)} %copy-done.2, bf16[1,2048,1024]{2,1,0:T(8,128)(2,1)} %local.1, f32[2048,1024]{1,0:T(8,128)} %anchor.3), custom_call_target="tpu_custom_call" | custom-call | tf_op jit(solution)/shard_map/mean/pallas_call | solution.py:336
  56.8 0.0 copy-done.1
  56.8 0.0 copy-done
  56.8 6.1 %update.1 = (f32[2048,1024]{1,0:T(8,128)}, f32[2048,256]{1,0:T(8,128)}) custom-call(s16[8,2,4,80,128]{4,3,2,1,0:T(8,128)(2,1)S(1)} %get-tuple-element.4.gathered, bf16[768,1024]{1,0:T(8,128)(2,1)S(1)} %get-tuple-element.5.turned, f32[2048,1024]{1,0:T(8,128)S(1)} %copy-done, f32[2048,256]{1,0:T(8,128)S(1)} %copy-done.1), custom_call_target="tpu_custom_call" | custom-call | tf_op jit(solution)/shard_map/update/pallas_call | solution.py:378
Async XLA Ops:
  0.6 56.2 %copy-start.1 = (f32[2048,256]{1,0:T(8,128)S(1)}, f32[2048,256]{1,0:T(8,128)}, u32[]{:S(2)}) copy-start(f32[2048,256]{1,0:T(8,128)} %momentum.1) | copy-start | bytes 6291460
  0.6 1.1 %copy-start.2 = (bf16[1,128,1024]{2,1,0:T(8,128)(2,1)S(1)}, bf16[1,128,1024]{2,1,0:T(8,128)(2,1)}, u32[]{:S(2)}) copy-start(bf16[1,128,1024]{2,1,0:T(8,128)(2,1)} %grads.1) | copy-start | bytes 786436
  1.7 0.7 %copy-start.3 = (s32[2]{0:T(128)S(1)}, s32[2]{0:T(128)}, u32[]{:S(2)}) copy-start(s32[2]{0:T(128)} %key_hbm.1) | copy-start | bytes 28
  2.4 54.4 %copy-start = (f32[2048,1024]{1,0:T(8,128)S(1)}, f32[2048,1024]{1,0:T(8,128)}, u32[]{:S(2)}) copy-start(f32[2048,1024]{1,0:T(8,128)} %anchor.3) | copy-start | bytes 25165828

commit v8 on v7

--- a/solution.py
+++ b/solution.py
@@ -12,6 +12,7 @@
 CHUNKS = 8
 AHEAD = 2
 GROUP = 2
+DIRECT = 2
 PAD = 16
 LANES = 128
 LEVELS = 32500.0
@@ -82,7 +83,7 @@
 def mean_kernel(
     n_rep, n_y, n_f, key_hbm, act, grads, local, anchor, gathered, turned,
     key, proj, columns, weights, own_anchor, base, total, pg, grads_in, y_out, y_in, z_out, z_in,
-    act_s, act_r, pg_s, pg_r, y1_s, y1_r, z1_s, z1_r, z2_s, z2_r, y2_s, y2_r, here,
+    act_s, act_r, pg_s, pg_r, y1_s, y1_r, z1_s, z1_r, z2_s, z2_r, y2_s, y2_r, x2_s, x2_r, here,
 ):
     n_z = n_rep // n_y
     chunks, tokens_all, width = columns.shape
@@ -96,16 +97,21 @@
     z, y = rep // n_y, rep % n_y
     other = n_y - 1 - y
     y_peer = {"replica": z * n_y + other}
+    relayed = chunks - DIRECT
 
     def z_peer(d):
         return {"replica": ((z + d) % n_z) * n_y + y}
+
+    def cross_peer(d):
+        return {"replica": ((z + d) % n_z) * n_y + other}
 
     barrier = pltpu.get_barrier_semaphore()
     for d in range(1, n_f):
         pl.semaphore_signal(barrier, inc=1, device_id={"fsdp": (f + d) % n_f}, device_id_type=MESH)
     for d in range(1, n_z):
         pl.semaphore_signal(barrier, inc=1, device_id=z_peer(d), device_id_type=MESH)
-    pl.semaphore_signal(barrier, inc=1, device_id=y_peer, device_id_type=MESH)
+    for d in range(n_z):
+        pl.semaphore_signal(barrier, inc=1, device_id=cross_peer(d), device_id_type=MESH)
 
     def remote(src, dst, send, recv, device):
         return pltpu.make_async_remote_copy(
@@ -156,6 +162,11 @@
 
     def y2_copy(c):
         return remote(gathered.at[c, y], gathered.at[c, y], y2_s.at[c], y2_r.at[c], y_peer)
+
+    def cross_copy(c, d):
+        return remote(
+            gathered.at[c, y, z], gathered.at[c, y, z], x2_s.at[c, d], x2_r.at[c, d], cross_peer(d)
+        )
 
     fetch = pltpu.make_async_copy(grads.at[0], grads_in, here.at[3, 0])
     fetch.start()
@@ -165,7 +176,7 @@
         weight_copy(c).start()
         act_own(c).start()
         anchor_copy(c).start()
-    pl.semaphore_wait(barrier, n_f + n_z - 1)
+    pl.semaphore_wait(barrier, n_f + 2 * n_z - 2)
     order = sorted(range(1, n_f), key=lambda d: abs(d - n_f // 2))
     for d in order:
         act_copy(0, d).start()
@@ -243,10 +254,18 @@
         for d in range(1, n_z):
             z2_copy(c, d).start()
 
+        @pl.when(c >= relayed)
+        def _():
+            for d in range(n_z):
+                cross_copy(c, d).start()
+
     def hand_over(c):
         for d in range(1, n_z):
             z2_copy(c, d).wait_recv()
-        y2_copy(c).start()
+
+        @pl.when(c < relayed)
+        def _():
+            y2_copy(c).start()
 
     stages = ((partial_sum, 0), (hand_over, 4), (sum_of_pair, 1), (whole_mean, 2))
 
@@ -269,8 +288,17 @@
         for d in range(1, n_z):
             z1_copy(c, d).wait_send()
             z2_copy(c, d).wait_send()
-        y2_copy(c).wait_send()
-        y2_copy(c).wait_recv()
+
+        @pl.when(c < relayed)
+        def _():
+            y2_copy(c).wait_send()
+            y2_copy(c).wait_recv()
+
+        @pl.when(c >= relayed)
+        def _():
+            for d in range(n_z):
+                cross_copy(c, d).wait_send()
+                cross_copy(c, d).wait_recv()
 
 
 def update_kernel(
@@ -367,6 +395,8 @@
             dma((CHUNKS, n_z - 1)),
             dma((CHUNKS,)),
             dma((CHUNKS,)),
+            dma((CHUNKS, n_z)),
+            dma((CHUNKS, n_z)),
             dma((4, CHUNKS)),
         ],
         compiler_params=pltpu.CompilerParams(

time: 63.1 us -> 63.4 us (level)
  no operation moved by 1% of the time
where the time goes in v8:
time: 63.4 us; the launch traced here: 63.2 us
  Pallas kernels  60.8 us (96%)
  local copies, waits for them, and re-layouts  1.75 us (3%)
  between operations  0.67 us (1%)
    pallas_call x1, Pallas kernels, in_kernels(): pl.pallas_call(functools.partial(mean_kernel, n_rep, n_y, n_f), out_shape...  54.7 us
    pallas_call x1, Pallas kernels, in_kernels(): pl.pallas_call(update_kernel, out_shape=(jax.ShapeDtypeStruct(anchor.shap...  6.09 us
    unnamed x8, local copies, waits for them, and re-layouts  1.75 us

profile of v8, /device:TPU:0, one launch (start us, length us, event | category | flops | bytes accessed | tf_op | source)
XLA Modules:
  0.0 63.2 jit_solution(9788391703064720035)
XLA Ops:
  0.6 0.0 copy-start.1
  0.6 0.0 copy-start.2
  0.7 1.1 %copy-done.2 = bf16[1,128,1024]{2,1,0:T(8,128)(2,1)S(1)} copy-done((bf16[1,128,1024]{2,1,0:T(8,128)(2,1)S(1)}, bf16[1,128,1024]{2,1,0:T(8,128)(2,1)}, u32[]{:S(2)}) %copy-start.2) | copy-done | bytes 262168
  1.7 0.0 copy-start.3
  1.7 0.7 %copy-done.3 = s32[2]{0:T(128)S(1)} copy-done((s32[2]{0:T(128)S(1)}, s32[2]{0:T(128)}, u32[]{:S(2)}) %copy-start.3) | copy-done | bytes 32
  2.4 0.0 copy-start
  2.4 54.7 %mean.1 = (s16[8,2,4,80,128]{4,3,2,1,0:T(8,128)(2,1)S(1)}, bf16[768,1024]{1,0:T(8,128)(2,1)S(1)}) custom-call(s32[2]{0:T(128)S(1)} %copy-done.3, bf16[1,128,8192]{2,1,0:T(8,128)(2,1)} %act.1, bf16[1,128,1024]{2,1,0:T(8,128)(2,1)S(1)} %copy-done.2, bf16[1,2048,1024]{2,1,0:T(8,128)(2,1)} %local.1, f32[2048,1024]{1,0:T(8,128)} %anchor.3), custom_call_target="tpu_custom_call" | custom-call | tf_op jit(solution)/shard_map/mean/pallas_call | solution.py:364
  57.1 0.0 copy-done.1
  57.1 0.0 copy-done
  57.1 6.1 %update.1 = (f32[2048,1024]{1,0:T(8,128)}, f32[2048,256]{1,0:T(8,128)}) custom-call(s16[8,2,4,80,128]{4,3,2,1,0:T(8,128)(2,1)S(1)} %get-tuple-element.4.gathered, bf16[768,1024]{1,0:T(8,128)(2,1)S(1)} %get-tuple-element.5.turned, f32[2048,1024]{1,0:T(8,128)S(1)} %copy-done, f32[2048,256]{1,0:T(8,128)S(1)} %copy-done.1), custom_call_target="tpu_custom_call" | custom-call | tf_op jit(solution)/shard_map/update/pallas_call | solution.py:408
Async XLA Ops:
  0.6 56.5 %copy-start.1 = (f32[2048,256]{1,0:T(8,128)S(1)}, f32[2048,256]{1,0:T(8,128)}, u32[]{:S(2)}) copy-start(f32[2048,256]{1,0:T(8,128)} %momentum.1) | copy-start | bytes 6291460
  0.6 1.1 %copy-start.2 = (bf16[1,128,1024]{2,1,0:T(8,128)(2,1)S(1)}, bf16[1,128,1024]{2,1,0:T(8,128)(2,1)}, u32[]{:S(2)}) copy-start(bf16[1,128,1024]{2,1,0:T(8,128)(2,1)} %grads.1) | copy-start | bytes 786436
  1.7 0.7 %copy-start.3 = (s32[2]{0:T(128)S(1)}, s32[2]{0:T(128)}, u32[]{:S(2)}) copy-start(s32[2]{0:T(128)} %key_hbm.1) | copy-start | bytes 28
  2.4 54.7 %copy-start = (f32[2048,1024]{1,0:T(8,128)S(1)}, f32[2048,1024]{1,0:T(8,128)}, u32[]{:S(2)}) copy-start(f32[2048,1024]{1,0:T(8,128)} %anchor.3) | copy-start | bytes 25165828

commit v9 on v7

--- a/solution.py
+++ b/solution.py
@@ -248,9 +248,9 @@
             z2_copy(c, d).wait_recv()
         y2_copy(c).start()
 
-    stages = ((partial_sum, 0), (hand_over, 4), (sum_of_pair, 1), (whole_mean, 2))
-
-    @pl.loop(0, chunks + 4)
+    stages = ((partial_sum, 0), (sum_of_pair, 1), (whole_mean, 2), (hand_over, 3))
+
+    @pl.loop(0, chunks + 3)
     def _(t):
         for stage, lag in stages:
 

time: 63.1 us -> 64.8 us (1.027)
  Pallas kernels: 60.5 us -> 62.2 us
    pallas_call x1, Pallas kernels: 54.4 us -> 56.1 us  [in_kernels(): pl.pallas_call(functools.partial(mean_kernel, n_rep, n_y, n_f), out_shape...]
where the time goes in v9:
time: 64.8 us; the launch traced here: 64.6 us
  Pallas kernels  62.2 us (96%)
  local copies, waits for them, and re-layouts  1.75 us (3%)
  between operations  0.67 us (1%)
    pallas_call x1, Pallas kernels, in_kernels(): pl.pallas_call(functools.partial(mean_kernel, n_rep, n_y, n_f), out_shape...  56.1 us
    pallas_call x1, Pallas kernels, in_kernels(): pl.pallas_call(update_kernel, out_shape=(jax.ShapeDtypeStruct(anchor.shap...  6.12 us
    unnamed x8, local copies, waits for them, and re-layouts  1.75 us

profile of v9, /device:TPU:0, one launch (start us, length us, event | category | flops | bytes accessed | tf_op | source)
XLA Modules:
  0.0 64.6 jit_solution(38301721122566588)
XLA Ops:
  0.6 0.0 copy-start.1
  0.6 0.0 copy-start.2
  0.7 1.1 %copy-done.2 = bf16[1,128,1024]{2,1,0:T(8,128)(2,1)S(1)} copy-done((bf16[1,128,1024]{2,1,0:T(8,128)(2,1)S(1)}, bf16[1,128,1024]{2,1,0:T(8,128)(2,1)}, u32[]{:S(2)}) %copy-start.2) | copy-done | bytes 262168
  1.7 0.0 copy-start.3
  1.7 0.7 %copy-done.3 = s32[2]{0:T(128)S(1)} copy-done((s32[2]{0:T(128)S(1)}, s32[2]{0:T(128)}, u32[]{:S(2)}) %copy-start.3) | copy-done | bytes 32
  2.4 0.0 copy-start
  2.4 56.1 %mean.1 = (s16[8,2,4,80,128]{4,3,2,1,0:T(8,128)(2,1)S(1)}, bf16[768,1024]{1,0:T(8,128)(2,1)S(1)}) custom-call(s32[2]{0:T(128)S(1)} %copy-done.3, bf16[1,128,8192]{2,1,0:T(8,128)(2,1)} %act.1, bf16[1,128,1024]{2,1,0:T(8,128)(2,1)S(1)} %copy-done.2, bf16[1,2048,1024]{2,1,0:T(8,128)(2,1)} %local.1, f32[2048,1024]{1,0:T(8,128)} %anchor.3), custom_call_target="tpu_custom_call" | custom-call | tf_op jit(solution)/shard_map/mean/pallas_call | solution.py:336
  58.5 0.0 copy-done.1
  58.5 0.0 copy-done
  58.5 6.1 %update.1 = (f32[2048,1024]{1,0:T(8,128)}, f32[2048,256]{1,0:T(8,128)}) custom-call(s16[8,2,4,80,128]{4,3,2,1,0:T(8,128)(2,1)S(1)} %get-tuple-element.4.gathered, bf16[768,1024]{1,0:T(8,128)(2,1)S(1)} %get-tuple-element.5.turned, f32[2048,1024]{1,0:T(8,128)S(1)} %copy-done, f32[2048,256]{1,0:T(8,128)S(1)} %copy-done.1), custom_call_target="tpu_custom_call" | custom-call | tf_op jit(solution)/shard_map/update/pallas_call | solution.py:378
Async XLA Ops:
  0.6 57.9 %copy-start.1 = (f32[2048,256]{1,0:T(8,128)S(1)}, f32[2048,256]{1,0:T(8,128)}, u32[]{:S(2)}) copy-start(f32[2048,256]{1,0:T(8,128)} %momentum.1) | copy-start | bytes 6291460
  0.6 1.1 %copy-start.2 = (bf16[1,128,1024]{2,1,0:T(8,128)(2,1)S(1)}, bf16[1,128,1024]{2,1,0:T(8,128)(2,1)}, u32[]{:S(2)}) copy-start(bf16[1,128,1024]{2,1,0:T(8,128)(2,1)} %grads.1) | copy-start | bytes 786436
  1.7 0.7 %copy-start.3 = (s32[2]{0:T(128)S(1)}, s32[2]{0:T(128)}, u32[]{:S(2)}) copy-start(s32[2]{0:T(128)} %key_hbm.1) | copy-start | bytes 28
  2.4 56.1 %copy-start = (f32[2048,1024]{1,0:T(8,128)S(1)}, f32[2048,1024]{1,0:T(8,128)}, u32[]{:S(2)}) copy-start(f32[2048,1024]{1,0:T(8,128)} %anchor.3) | copy-start | bytes 25165828
